TPU v7x, 256 devices: a whole 4x4x8 slice. The times are simulated.
256 devices in a mesh: patch: 64 (over y, z, core), sub: 4 (over x).
Axes of the slice: x: 4, y: 4, z: 8, core: 2. Of those that a mesh axis runs over, the one named last changes fastest.
Arguments:
- positions: float32 [3, 8192, 128], P(None, 'patch'), may hold values from 0 to 24, as said below
- velocities: float32 [3, 8192, 128], P(None, 'patch'), may hold values from -0.3 to 0.3
- charges: float32 [8192, 128], P('patch'), may hold values from -1.2 to 1.2
- atom_type: int32 [8192, 128], P('patch'), may hold values from 0 to 7
- patch_fill: int32 [8192], P('patch'), may hold values from 8 to 128, as said below
- sigma_table: float32 [8], replicated, may hold values from 2.5 to 3.2
- eps_table: float32 [8], replicated, may hold values from 0.05 to 0.3
- inv_mass_table: float32 [8], replicated, may hold values from 0.3 to 1
- pair_first: int32 [64, 4, 896], P('patch', 'sub'), may hold values from 0 to 8191, as said below
- pair_second: int32 [64, 4, 896], P('patch', 'sub'), may hold values from -1 to 8191, as said below
Outputs:
- new_velocities: float32 [3, 8192, 128], P(None, 'patch')
- new_positions: float32 [3, 8192, 128], P(None, 'patch')
Inputs may be any that keep to these rules, and one draw needn't show every extreme that they name: `positions`: every coordinate lies within its patch's cell; any two atoms, in one patch or in neighbouring ones, are 2.6 or more apart. `patch_fill`: some patch is full in every draw. All slots of device (g, s), live or not, have pair_first in one layer h, which is g - 1, g or g + 1 (modulo 64); for a live slot the cell step from pair_first to pair_second is (dx, dy, 1) with dx, dy in -1, 0, 1, or (0, 0, 0), (1, 0, 0), (-1, 1, 0), (0, 1, 0) or (1, 1, 0); every patch with itself and every two patches whose cells touch are in exactly one live slot; for each s, the slots whose pair_first lies in layer h sit on one device (., s). `pair_second`: same slots as pair_first; on each device the live slots come first and the unused ones hold -1; some device has all 896 slots live.
All inputs are finite; a program needn't handle non-finite values.
Results may differ from a plain program's by a relative error of at most 0.0003.
Values sent between devices are 32-bit elements; how exact they have to be, the bound alone decides.
A program may use at most 64 MiB of HBM per device.

v0:
```python
import math

import jax
import jax.numpy as jnp
from jax import lax
from jax.sharding import PartitionSpec as P

PX = 8


COULOMB = 332.0636
SPLIT_BETA = 0.2
GAUSS_FACTOR = 2.0 * 0.2 / math.sqrt(math.pi)
CUTOFF_SQ = 144.0
KICK_SCALE = 0.04
CELL_WIDTH = 12.0
CELL_HEIGHT = 24.0


def shifted(value, axis, steps):
    count = lax.axis_size(axis)
    pairs = [(source, (source + steps) % count) for source in range(count)]
    return lax.ppermute(value, axis, pairs)


def atom_features(positions, charges, atom_type, patch_fill, sigma_table, eps_table):
    onehot = (
        atom_type[None] == jnp.arange(sigma_table.shape[0], dtype=jnp.int32)[:, None, None]
    ).astype(jnp.float32)
    sigma = jnp.sum(onehot * sigma_table[:, None, None], axis=0)
    depth = jnp.sum(onehot * jnp.sqrt(eps_table)[:, None, None], axis=0)
    present = jnp.arange(charges.shape[1], dtype=jnp.int32)[None, :] < patch_fill[:, None]
    features = jnp.stack(
        [
            positions[0],
            positions[1],
            positions[2],
            jnp.where(present, charges, 0.0),
            sigma,
            jnp.where(present, depth, 0.0),
        ]
    )
    return (features, onehot)


def cell_shift(first_patch, second_patch, patches, width_cells, layers):
    depth_cells = patches // width_cells
    first_within = first_patch % patches
    second_within = second_patch % patches
    step_x = (
        second_within % width_cells - first_within % width_cells + 1 + width_cells
    ) % width_cells - 1
    step_y = (
        second_within // width_cells - first_within // width_cells + 1 + depth_cells
    ) % depth_cells - 1
    step_z = (second_patch // patches - first_patch // patches + 1 + layers) % layers - 1
    return (
        CELL_WIDTH * step_x.astype(jnp.float32),
        CELL_WIDTH * step_y.astype(jnp.float32),
        CELL_HEIGHT * step_z.astype(jnp.float32),
    )


def pair_block(first_atoms, second_atoms, shift, self_pair):
    delta_x = first_atoms[0][:, :, None] - second_atoms[0][:, None, :] - shift[0][:, None, None]
    delta_y = first_atoms[1][:, :, None] - second_atoms[1][:, None, :] - shift[1][:, None, None]
    delta_z = first_atoms[2][:, :, None] - second_atoms[2][:, None, :] - shift[2][:, None, None]
    dist_sq = delta_x * delta_x + delta_y * delta_y + delta_z * delta_z
    slots = jnp.arange(first_atoms.shape[2], dtype=jnp.int32)
    excluded = jnp.logical_and(self_pair[:, None, None], (slots[:, None] == slots[None, :])[None])
    dist_sq = jnp.where(excluded, 1.0, dist_sq)
    within = jnp.logical_and(dist_sq < CUTOFF_SQ, jnp.logical_not(excluded))
    inverse_sq = 1.0 / dist_sq
    distance = jnp.sqrt(dist_sq)
    sigma_pair = 0.5 * (first_atoms[4][:, :, None] + second_atoms[4][:, None, :])
    ratio_two = sigma_pair * sigma_pair * inverse_sq
    ratio_six = ratio_two * ratio_two * ratio_two
    depth_pair = first_atoms[5][:, :, None] * second_atoms[5][:, None, :]
    dispersion = 24.0 * depth_pair * (2.0 * ratio_six * ratio_six - ratio_six) * inverse_sq
    charge_pair = COULOMB * first_atoms[3][:, :, None] * second_atoms[3][:, None, :]
    screened = (
        charge_pair
        * (
            jax.scipy.special.erfc(SPLIT_BETA * distance) / distance
            + GAUSS_FACTOR * jnp.exp(-SPLIT_BETA * SPLIT_BETA * dist_sq)
        )
        * inverse_sq
    )
    magnitude = jnp.where(within, dispersion + screened, 0.0)
    pull_x = magnitude * delta_x
    pull_y = magnitude * delta_y
    pull_z = magnitude * delta_z
    on_first = jnp.stack(
        [jnp.sum(pull_x, axis=2), jnp.sum(pull_y, axis=2), jnp.sum(pull_z, axis=2)]
    )
    on_second = -jnp.stack(
        [jnp.sum(pull_x, axis=1), jnp.sum(pull_y, axis=1), jnp.sum(pull_z, axis=1)]
    )
    return (on_first, on_second)


def pair_partials(window, base_group, span, firsts, raw_seconds, patches, layers):
    width = window.shape[2]
    block_slots = 24
    count = firsts.shape[0]
    live = jnp.sum((raw_seconds >= 0).astype(jnp.int32))
    seconds = jnp.where(raw_seconds >= 0, raw_seconds, firsts)
    padded = -(-count // block_slots) * block_slots
    firsts = jnp.concatenate([firsts, jnp.full((padded - count,), firsts[0], jnp.int32)])
    seconds = jnp.concatenate([seconds, jnp.full((padded - count,), seconds[0], jnp.int32)])

    def place(patch):
        return (patch // patches - base_group + layers) % layers * patches + patch % patches

    def apply_block(turn, totals):
        start = turn * block_slots
        first_patch = lax.dynamic_slice_in_dim(firsts, start, block_slots)
        second_patch = lax.dynamic_slice_in_dim(seconds, start, block_slots)
        first_local = place(first_patch)
        second_local = place(second_patch)
        first_atoms = jnp.take(window, first_local, axis=1)
        second_atoms = jnp.take(window, second_local, axis=1)
        shift = cell_shift(first_patch, second_patch, patches, PX, layers)
        self_pair = first_patch == second_patch
        on_first, on_second = pair_block(first_atoms, second_atoms, shift, self_pair)
        active = (start + jnp.arange(block_slots, dtype=jnp.int32) < live).astype(jnp.float32)
        weight_second = jnp.where(self_pair, 0.0, active)
        totals = totals.at[:, first_local, :].add(on_first * active[None, :, None])
        return totals.at[:, second_local, :].add(on_second * weight_second[None, :, None])

    turns = (live + block_slots - 1) // block_slots
    return lax.fori_loop(0, turns, apply_block, jnp.zeros((3, span * patches, width), jnp.float32))


def local(
    positions,
    velocities,
    charges,
    atom_type,
    patch_fill,
    sigma_table,
    eps_table,
    inv_mass_table,
    pair_first,
    pair_second,
):
    patches = positions.shape[1]
    width = positions.shape[2]
    layers = lax.axis_size("patch")
    own_group = lax.axis_index("patch")
    features, onehot = atom_features(
        positions, charges, atom_type, patch_fill, sigma_table, eps_table
    )
    offsets = (-1, 1, 2)
    arrived = {}
    for offset in offsets:
        arrived[offset] = shifted(features, "patch", -offset)
    window = jnp.concatenate([arrived[-1], features, arrived[1], arrived[2]], axis=1)
    partial_value = pair_partials(
        window, own_group - 1, 4, pair_first[0, 0], pair_second[0, 0], patches, layers
    )
    blocks = partial_value.reshape(3, 4, patches, width)
    gathered = blocks[:, 1]
    for offset in offsets:
        gathered = gathered + shifted(blocks[:, offset + 1], "patch", offset)
    forces = lax.psum(gathered, "sub")
    inverse_mass = jnp.sum(onehot * inv_mass_table[:, None, None], axis=0)
    new_velocities = velocities + KICK_SCALE * inverse_mass[None] * forces
    new_positions = positions + new_velocities
    return (new_velocities, new_positions)


def solution(mesh):
    return jax.shard_map(
        local,
        mesh=mesh,
        in_specs=(
            P(None, "patch", None),
            P(None, "patch", None),
            P("patch", None),
            P("patch", None),
            P("patch"),
            P(),
            P(),
            P(),
            P("patch", "sub", None),
            P("patch", "sub", None),
        ),
        out_specs=(P(None, "patch", None), P(None, "patch", None)),
        check_vma=False,
    )
```

profile of v0, /device:TPU:2, one launch (start us, length us, event | category | flops | bytes accessed | tf_op | source)
XLA Modules:
  0.0 645.1 jit_solution(16967856151210818016)
XLA Ops:
  7.2 0.7 sqrt.10
  7.9 0.9 fusion.51
  8.8 1.1 select_reduce_fusion.2
  9.9 0.7 bitcast_select_fusion
  10.6 1.1 copy.19
  12.0 8.4 %collective-permute-start.2 = (f32[6,128,128]{2,0,1:T(8,128)S(1)}, f32[6,128,128]{2,0,1:T(8,128)S(1)}, u32[]{:S(2)}, u32[]{:S(2)}) collective-permute-start(f32[6,128,128]{2,0,1:T(8,128)S(1)} %pad_maximum_fusion.1), channel_id=1, source_target_pairs={{0,248},{4,252},{8,0},{12,4},{16,8},{20,12},{24,16},{28,20},{32,24... | collective-permute-start | bytes 1179656 | tf_op jit(solution)/shard_map/ppermute | solution.py:23
  20.5 0.3 collective-permute-start
  20.9 0.6 slice.107
  21.5 0.6 compare_select_fusion.24
  22.8 0.7 concatenate.9
  23.5 0.6 slice.108
  24.1 0.7 concatenate.10
  24.8 6.7 %collective-permute-done.2 = f32[6,128,128]{2,0,1:T(8,128)S(1)} collective-permute-done((f32[6,128,128]{2,0,1:T(8,128)S(1)}, f32[6,128,128]{2,0,1:T(8,128)S(1)}, u32[]{:S(2)}, u32[]{:S(2)}) %collective-permute-start.2) | collective-permute-done | bytes 393248 | tf_op jit(solution)/shard_map/ppermute | solution.py:23
  31.5 5.6 collective-permute-done.1
  37.1 0.8 copy-done.2
  38.0 1.7 pad_maximum_fusion
  39.9 57.0 %while.13 = (s32[]{:T(128)}, f32[3,512,128]{2,0,1:T(4,128)S(1)}, s32[]{:T(128)}, s32[912]{0:T(1024)S(1)}, s32[]{:T(128)}, /*index=5*/s32[912]{0:T(1024)S(1)}, f3...) while((s32[]{:T(128)}, f32[3,512,128]{2,0,1:T(4,128)S(1)}, ...), condition=%wide.region_13.15_spmd, body=%wide.region_4.14_spmd.sunk | while | flops 42595276 | bytes 1666375 | solution.py:132
  40.0 0.7 broadcast_select_fusion.2
  40.8 0.6 gather_fusion
  41.6 0.6 gather_fusion.1
  42.3 8.2 %fusion.65 = (f32[24,128]{1,0:T(8,128)S(1)}, f32[24,128]{1,0:T(8,128)S(1)}, f32[24,128]{1,0:T(8,128)S(1)}, f32[24,128]{1,0:T(8,128)S(1)}, f32[24,128]{1,0:T(8,128)S(1)}, /*index=5*/f32[24,128]{1,0:T(8,128)S(1)}) fusion(f32[24]{0:T(128)S(1)} %get-tuple-element.321, f32[24,128]{1,0:T(8,128)S(1)} %bitcast.113, f32[24,128]{1,0:T(8,128)S(1)} %bitcast.122, ...), kind=kLoop, calls=%fused_computation.40.clone.1 | loop fusion | flops 42448896 | bytes 237880 | tf_op jit(solution)/shard_map/while/body/reduce_sum | solution.py:97
  50.7 1.7 scatter_fusion
  52.4 1.7 scatter_fusion.1
  54.2 0.7 broadcast_select_fusion.2
  55.1 0.6 gather_fusion
  55.8 0.6 gather_fusion.1
  56.6 8.2 %fusion.65 = (f32[24,128]{1,0:T(8,128)S(1)}, f32[24,128]{1,0:T(8,128)S(1)}, f32[24,128]{1,0:T(8,128)S(1)}, f32[24,128]{1,0:T(8,128)S(1)}, f32[24,128]{1,0:T(8,128)S(1)}, /*index=5*/f32[24,128]{1,0:T(8,128)S(1)}) fusion(f32[24]{0:T(128)S(1)} %get-tuple-element.321, f32[24,128]{1,0:T(8,128)S(1)} %bitcast.113, f32[24,128]{1,0:T(8,128)S(1)} %bitcast.122, ...), kind=kLoop, calls=%fused_computation.40.clone.1 | loop fusion | flops 42448896 | bytes 237880 | tf_op jit(solution)/shard_map/while/body/reduce_sum | solution.py:97
  64.9 1.7 scatter_fusion
  66.6 1.7 scatter_fusion.1
  68.5 0.7 broadcast_select_fusion.2
  69.3 0.6 gather_fusion
  70.0 0.6 gather_fusion.1
  70.8 8.2 %fusion.65 = (f32[24,128]{1,0:T(8,128)S(1)}, f32[24,128]{1,0:T(8,128)S(1)}, f32[24,128]{1,0:T(8,128)S(1)}, f32[24,128]{1,0:T(8,128)S(1)}, f32[24,128]{1,0:T(8,128)S(1)}, /*index=5*/f32[24,128]{1,0:T(8,128)S(1)}) fusion(f32[24]{0:T(128)S(1)} %get-tuple-element.321, f32[24,128]{1,0:T(8,128)S(1)} %bitcast.113, f32[24,128]{1,0:T(8,128)S(1)} %bitcast.122, ...), kind=kLoop, calls=%fused_computation.40.clone.1 | loop fusion | flops 42448896 | bytes 237880 | tf_op jit(solution)/shard_map/while/body/reduce_sum | solution.py:97
  79.2 1.7 scatter_fusion
  80.9 1.7 scatter_fusion.1
  82.7 0.7 broadcast_select_fusion.2
  83.5 0.6 gather_fusion
  84.3 0.6 gather_fusion.1
  85.0 8.2 %fusion.65 = (f32[24,128]{1,0:T(8,128)S(1)}, f32[24,128]{1,0:T(8,128)S(1)}, f32[24,128]{1,0:T(8,128)S(1)}, f32[24,128]{1,0:T(8,128)S(1)}, f32[24,128]{1,0:T(8,128)S(1)}, /*index=5*/f32[24,128]{1,0:T(8,128)S(1)}) fusion(f32[24]{0:T(128)S(1)} %get-tuple-element.321, f32[24,128]{1,0:T(8,128)S(1)} %bitcast.113, f32[24,128]{1,0:T(8,128)S(1)} %bitcast.122, ...), kind=kLoop, calls=%fused_computation.40.clone.1 | loop fusion | flops 42448896 | bytes 237880 | tf_op jit(solution)/shard_map/while/body/reduce_sum | solution.py:97
  93.4 1.7 scatter_fusion
  95.1 1.7 scatter_fusion.1
  97.0 48.0 %collective-permute-start.3 = (f32[3,128,128]{2,1,0:T(8,128)S(1)}, f32[3,128,128]{2,1,0:T(8,128)S(1)}, u32[]{:S(2)}, u32[]{:S(2)}) collective-permute-start(f32[3,128,128]{2,1,0:T(8,128)S(1)} %get-tuple-element.229), channel_id=1, source_target_pairs={{0,252},{4,0},{8,4},{12,8},{16,12},{20,16},{24,20},{28,24},{32,28}... | collective-permute-start | bytes 589832 | tf_op jit(solution)/shard_map/ppermute | solution.py:23
  145.0 429.9 %collective-permute-start.5 = (f32[3,128,128]{2,1,0:T(8,128)S(1)}, f32[3,128,128]{2,1,0:T(8,128)S(1)}, u32[]{:S(2)}, u32[]{:S(2)}) collective-permute-start(f32[3,128,128]{2,1,0:T(8,128)S(1)} %get-tuple-element.230), channel_id=1, source_target_pairs={{0,8},{4,12},{8,16},{12,20},{16,24},{20,28},{24,32},{28,36},{32,40... | collective-permute-start | bytes 589832 | tf_op jit(solution)/shard_map/ppermute | solution.py:23
  575.1 5.1 collective-permute-done.5
  580.1 3.2 collective-permute-done.4
  583.3 0.7 fusion.50
  584.1 52.4 %all-reduce.4.cloned.1.call-done = f32[3,128,128]{2,1,0:T(8,128)} async-done(((f32[3,128,128]{2,1,0:T(8,128)}), f32[3,128,128]{2,1,0:T(8,128)}) %all-reduce.4.cloned.1.call-update) | async-done | bytes 196624 | tf_op jit(solution)/shard_map/psum | solution.py:166
  636.5 1.7 fusion.53
  (76 shorter events, 3.4 us)
Async XLA Ops:
  7.2 13.7 %copy-start.4 = (s32[1,1,896]{2,1,0:T(1,128)S(1)}, s32[1,1,896]{2,1,0:T(1,128)}, u32[]{:S(2)}) copy-start(s32[1,1,896]{2,1,0:T(1,128)} %param.22) | copy-start | bytes 10756
  7.2 14.3 %copy-start.5 = (s32[1,1,896]{2,1,0:T(1,128)S(1)}, s32[1,1,896]{2,1,0:T(1,128)}, u32[]{:S(2)}) copy-start(s32[1,1,896]{2,1,0:T(1,128)} %param.23) | copy-start | bytes 10756
  7.2 629.3 %all-reduce.4.cloned.1.call-start = ((), (), s32[]{:S(2)}) async-start(), calls=%async_computation | async-start | bytes 393216 | tf_op jit(solution)/shard_map/psum | solution.py:166
  12.0 19.6 %collective-permute-start.2 = (f32[6,128,128]{2,0,1:T(8,128)S(1)}, f32[6,128,128]{2,0,1:T(8,128)S(1)}, u32[]{:S(2)}, u32[]{:S(2)}) collective-permute-start(f32[6,128,128]{2,0,1:T(8,128)S(1)} %pad_maximum_fusion.1), channel_id=1, source_target_pairs={{0,248},{4,252},{8,0},{12,4},{16,8},{20,12},{24,16},{28,20},{32,24... | collective-permute-start | bytes 1179656 | tf_op jit(solution)/shard_map/ppermute | solution.py:23
  20.3 16.8 %collective-permute-start.1 = (f32[6,128,128]{2,0,1:T(8,128)S(1)}, f32[6,128,128]{2,0,1:T(8,128)S(1)}, u32[]{:S(2)}, u32[]{:S(2)}) collective-permute-start(f32[6,128,128]{2,0,1:T(8,128)S(1)} %pad_maximum_fusion.1), channel_id=1, source_target_pairs={{0,252},{4,0},{8,4},{12,8},{16,12},{20,16},{24,20},{28,24},{32,28}... | collective-permute-start | bytes 1179656 | tf_op jit(solution)/shard_map/ppermute | solution.py:23
  20.5 17.5 %collective-permute-start = (f32[6,128,128]{2,0,1:T(8,128)S(1)}, f32[6,128,128]{2,0,1:T(8,128)}, u32[]{:S(2)}, u32[]{:S(2)}) collective-permute-start(f32[6,128,128]{2,0,1:T(8,128)S(1)} %pad_maximum_fusion.1), channel_id=1, source_target_pairs={{0,4},{4,8},{8,12},{12,16},{16,20},{20,24},{24,28},{28,32},{32,36}... | collective-permute-start | bytes 1179656 | tf_op jit(solution)/shard_map/ppermute | solution.py:23
  31.5 5.6 copy-start.1
  37.1 0.8 copy-start.2
  96.9 539.6 %copy-start = (f32[3,128,128]{2,1,0:T(8,128)S(1)}, f32[3,128,128]{2,1,0:T(8,128)}, u32[]{:S(2)}) copy-start(f32[3,128,128]{2,1,0:T(8,128)} %param.14) | copy-start | bytes 589828
  96.9 539.6 %copy-start.3 = (f32[3,128,128]{2,1,0:T(8,128)S(1)}, f32[3,128,128]{2,1,0:T(8,128)}, u32[]{:S(2)}) copy-start(f32[3,128,128]{2,1,0:T(8,128)} %param.15) | copy-start | bytes 589828
  97.0 478.1 %collective-permute-start.3 = (f32[3,128,128]{2,1,0:T(8,128)S(1)}, f32[3,128,128]{2,1,0:T(8,128)S(1)}, u32[]{:S(2)}, u32[]{:S(2)}) collective-permute-start(f32[3,128,128]{2,1,0:T(8,128)S(1)} %get-tuple-element.229), channel_id=1, source_target_pairs={{0,252},{4,0},{8,4},{12,8},{16,12},{20,16},{24,20},{28,24},{32,28}... | collective-permute-start | bytes 589832 | tf_op jit(solution)/shard_map/ppermute | solution.py:23
  145.0 435.1 %collective-permute-start.5 = (f32[3,128,128]{2,1,0:T(8,128)S(1)}, f32[3,128,128]{2,1,0:T(8,128)S(1)}, u32[]{:S(2)}, u32[]{:S(2)}) collective-permute-start(f32[3,128,128]{2,1,0:T(8,128)S(1)} %get-tuple-element.230), channel_id=1, source_target_pairs={{0,8},{4,12},{8,16},{12,20},{16,24},{20,28},{24,32},{28,36},{32,40... | collective-permute-start | bytes 589832 | tf_op jit(solution)/shard_map/ppermute | solution.py:23
  574.9 8.4 %collective-permute-start.4 = (f32[3,128,128]{2,1,0:T(8,128)S(1)}, f32[3,128,128]{2,1,0:T(8,128)S(1)}, u32[]{:S(2)}, u32[]{:S(2)}) collective-permute-start(f32[3,128,128]{2,1,0:T(8,128)S(1)} %get-tuple-element.231), channel_id=1, source_target_pairs={{0,4},{4,8},{8,12},{12,16},{16,20},{20,24},{24,28},{28,32},{32,36}... | collective-permute-start | bytes 589832 | tf_op jit(solution)/shard_map/ppermute | solution.py:23
Sparse Core Ops, SparseCore 0:
  584.2 52.2 all-reduce.3
where the time goes:
time: 648 us; the launch traced here: 645 us
  starting transfers between devices  487 us (75%)
  waiting for transfers between devices  73 us (11%)
  other arithmetic  59.3 us (9%)
  between operations  14.9 us (2%)
  local copies, waits for them, and re-layouts  10.3 us (2%)
    ppermute x6, starting transfers between devices, shifted(): return lax.ppermute(value, axis, pairs)  487 us
    psum x1, waiting for transfers between devices, local(): forces = lax.psum(gathered, 'sub')  52.4 us
    reduce_sum x4, other arithmetic, pair_block(): jnp.sum(pull_x, axis=1)  32.7 us
    ppermute x6, waiting for transfers between devices, shifted(): return lax.ppermute(value, axis, pairs)  20.6 us
  transfers between devices with their start and end apart: 7, of which 5 were waited for; matrix products, arithmetic and copies ran while one was open for 1% of the time, Pallas kernels for 0%

commit v1 on v0

v1 whole, which is shorter than its diff:
```python
import math

import jax
import jax.numpy as jnp
from jax import lax
from jax.experimental import pallas as pl
from jax.experimental.pallas import tpu as pltpu
from jax.sharding import PartitionSpec as P

PX = 8
EXT = 48
OWN = 32
SUBS = 4
VMEM_BYTES = 48 * 1024 * 1024
GROUP = 2
UNROLL = 4
COULOMB = 332.0636
SPLIT_BETA = 0.2
CUTOFF_SQ = 144.0
KICK_SCALE = 0.04
CELL_WIDTH = 12.0
CELL_HEIGHT = 24.0
STEP_W = SPLIT_BETA * CELL_WIDTH
STEP_H = SPLIT_BETA * CELL_HEIGHT
CUT = SPLIT_BETA * SPLIT_BETA * CUTOFF_SQ
GAUSS = 2.0 / math.sqrt(math.pi)
LOG2E = math.log2(math.e)
SIGMA_SCALE = SPLIT_BETA * 0.5 * 2.0 ** (1.0 / 6.0)
DEPTH_SCALE = math.sqrt(12.0 * SPLIT_BETA)
CHARGE_SCALE = math.sqrt(COULOMB * SPLIT_BETA * SPLIT_BETA)
FAR = 1.0e4
PARTS = 2
MESH = pl.DeviceIdType.MESH
F32 = jnp.float32
BF16 = jnp.bfloat16


def split3(value):
    high = value.astype(BF16)
    rest = value - high.astype(F32)
    mid = rest.astype(BF16)
    low = (rest - mid.astype(F32)).astype(BF16)
    return high, mid, low


def lookup(kind, table_ref, scale, root):
    value = jnp.zeros(kind.shape, F32)
    for t in range(8):
        value = jnp.where(kind == t, table_ref[0:1, t : t + 1], value)
    if root:
        value = jnp.sqrt(value)
    return value * scale


def prep_kernel(
    pos_ref,
    charge_ref,
    type_ref,
    fill_ref,
    sigma_ref,
    eps_ref,
    fj_ref,
    fu_ref,
    rank_ref,
    low_ref,
    feat_ref,
    place_ref,
    send_sem,
    recv_sem,
):
    group = lax.axis_index("patch")
    groups = lax.axis_size("patch")
    below = lax.rem(group + groups - 1, groups)
    above = lax.rem(group + 1, groups)
    barrier = pltpu.get_barrier_semaphore()
    pl.semaphore_signal(barrier, inc=1, device_id={"patch": above}, device_id_type=MESH)
    lane = lax.broadcasted_iota(jnp.int32, (128, 128), 1)
    row = lax.broadcasted_iota(jnp.int32, (128, 128), 0)
    fill = jnp.broadcast_to(fill_ref[0:1, :].astype(F32), (128, 128)).T
    present = lane.astype(F32) < fill
    kind = type_ref[...]
    z = pos_ref[2]
    feat_ref[0:128] = jnp.where(present, pos_ref[0] * SPLIT_BETA, -FAR)
    feat_ref[128:256] = pos_ref[1] * SPLIT_BETA
    feat_ref[256:384] = z * SPLIT_BETA
    feat_ref[384:512] = jnp.where(present, charge_ref[...] * CHARGE_SCALE, 0.0)
    feat_ref[512:640] = lookup(kind, sigma_ref, SIGMA_SCALE, False)
    feat_ref[640:768] = jnp.where(present, lookup(kind, eps_ref, DEPTH_SCALE, True), 0.0)
    feat_ref[768:896] = jnp.where(present, pos_ref[0] * SPLIT_BETA, FAR)
    feat_ref[896:1024] = jnp.zeros((128, 128), F32)
    low = jnp.logical_and(present, z < 0.5 * CELL_HEIGHT).astype(F32)
    high = jnp.logical_and(present, z >= 0.5 * CELL_HEIGHT).astype(F32)
    upto = (row <= lane).astype(F32).astype(BF16)
    low_upto = jnp.dot(low.astype(BF16), upto, preferred_element_type=F32)
    high_upto = jnp.dot(high.astype(BF16), upto, preferred_element_type=F32)
    low_count = jnp.sum(low, axis=1, keepdims=True)
    place_ref[...] = jnp.where(
        low > 0.0,
        low_upto - 1.0,
        jnp.where(high > 0.0, low_count + high_upto - 1.0, lane.astype(F32)),
    )
    counts = lax.dot_general(
        jnp.ones((8, 128), BF16), low.astype(BF16), (((1,), (1,)), ((), ())), preferred_element_type=F32
    )
    low_ref[...] = counts.astype(jnp.int32)
    first = lax.axis_index("sub") * OWN - PX + 128
    slot = row.astype(F32)

    def one(k, carry):
        p = (first + k) & 127
        place = place_ref[pl.ds(p, 1), :]
        rank_ref[pl.ds(k, 1), :] = place
        hit = (place == slot).astype(F32).astype(BF16)
        tile = feat_ref[pl.ds(p, 8, stride=128), :]
        total = jnp.zeros((8, 128), F32)
        for part in split3(tile):
            total = total + lax.dot_general(
                part, hit, (((1,), (1,)), ((), ())), preferred_element_type=F32
            )
        fj_ref[k] = total
        return carry

    pl.semaphore_wait(barrier, 1)
    copies = []
    for part in range(PARTS):
        size = EXT // PARTS
        lax.fori_loop(part * size, (part + 1) * size, one, 0, unroll=4)
        copy = pltpu.make_async_remote_copy(
            src_ref=fj_ref.at[pl.ds(part * size, size)],
            dst_ref=fu_ref.at[pl.ds(part * size, size)],
            send_sem=send_sem.at[part],
            recv_sem=recv_sem.at[part],
            device_id={"patch": below},
            device_id_type=MESH,
        )
        copy.start()
        copies.append(copy)
    for copy in copies:
        copy.wait()


def unit(lead, ref, b, own=None):
    xi, yi, zi, qi, si, ei = lead
    dx = xi - ref[b, 0:1, :]
    dy = yi - ref[b, 1:2, :]
    dz = zi - ref[b, 2:3, :]
    v = dx * dx + dy * dy + dz * dz
    if own is not None:
        v = jnp.where(own, 2.0 * CUT, v)
    w = lax.rsqrt(v)
    w2 = w * w
    u = (si + ref[b, 4:5, :]) * w
    u = u * u
    u = u * u * u
    screened = (1.0 - lax.erf(v * w)) * w + GAUSS * jnp.exp2(v * (-LOG2E))
    both = (ei * ref[b, 5:6, :]) * (u * u - u) + (qi * ref[b, 3:4, :]) * screened
    m = jnp.where(v < CUT, both * w2, 0.0)
    return m * dx, m * dy, m * dz


def pair_kernel(
    sub_ref, fill_ref, low_ref, fj_ref, fu_ref, own_ref, up_ref, lead_ref, blk_ref, a1_ref, acc_ref, accu_ref
):
    lane8 = lax.broadcasted_iota(jnp.int32, (8, 128), 1)
    row8 = lax.broadcasted_iota(jnp.int32, (8, 128), 0)
    half = lane8 < 64
    first = sub_ref[0] * OWN - PX + 128

    def clear(k, carry):
        acc_ref[k] = jnp.zeros((24, 128), F32)
        accu_ref[k] = jnp.zeros((24, 128), F32)
        return carry

    lax.fori_loop(0, EXT, clear, 0)
    own_ref[...] = jnp.zeros((3, EXT, 128), F32)

    def pack(p, worst):
        even = fu_ref[2 * p]
        odd = fu_ref[2 * p + 1]
        worst = jnp.maximum(worst, jnp.where(even[0:1] > -1.0, 0.5 * STEP_H - even[2:3], 0.0))
        worst = jnp.maximum(worst, jnp.where(odd[0:1] > -1.0, 0.5 * STEP_H - odd[2:3], 0.0))
        odd = jnp.where(row8 == 0, odd + STEP_W, odd)
        blk_ref[p] = jnp.where(half, even, pltpu.roll(odd, 64, 1))
        blk_ref[24 + p] = jnp.where(half, pltpu.roll(even, 64, 1), odd)
        return worst

    worst = lax.fori_loop(0, 24, pack, jnp.zeros((1, 128), F32))
    spill = jnp.max(jnp.where(lane8[0:1] >= 64, worst, 0.0)) > 0.0

    def lead_of(k, c):
        return tuple(lead_ref[k, f, pl.ds(c * 8, 8), :] for f in range(6))

    def add(total, term):
        return tuple(t + u for t, u in zip(total, term))

    def drain(ref, b, total):
        for d in range(3):
            ref[b, 8 * d : 8 * d + 8, :] -= total[d]

    def plane_units(ia, x, c, leads):
        left = ia - x + ((x + 7) & 7)
        right = ia - x + ((x + 1) & 7)
        force = [unit(lead, fj_ref, ia, (row8 + (c + n) * 8) == lane8) for n, lead in enumerate(leads)]
        for sx, sy, b in ((1, 0, right), (-1, 1, left + PX), (0, 1, ia + PX), (1, 1, right + PX)):
            total = None
            for n, (xi, yi, zi, qi, si, ei) in enumerate(leads):
                xs = xi - sx * STEP_W if sx else xi
                ys = yi - sy * STEP_W if sy else yi
                term = unit((xs, ys, zi, qi, si, ei), fj_ref, b)
                force[n] = add(force[n], term)
                total = term if total is None else add(total, term)
            drain(acc_ref, b, total)
        return force

    def up_units(ia, x, leads, base, force):
        shift = STEP_W * (x & 1).astype(F32)
        p1 = (x + 1) // 2
        p0 = (p1 + 3) & 3
        p1 = p1 & 3
        r = ia // PX
        for dr in (-1, 0, 1):
            for side, p in ((2.0 * STEP_W, p0), (0.0, p1)):
                b = base + (r + dr) * 4 + p
                total = None
                for n, (xi, yi, zi, qi, si, ei) in enumerate(leads):
                    term = unit((xi + (side - shift), yi - STEP_W * dr, zi - STEP_H, qi, si, ei), blk_ref, b)
                    force[n] = add(force[n], term)
                    total = term if total is None else add(total, term)
                drain(accu_ref, b, total)
        return force

    def put(k, c, force):
        for n, total in enumerate(force):
            for d in range(3):
                a1_ref[k, d, pl.ds((c + n) * 8, 8), :] = total[d]

    def spread(k, carry):
        turned = fj_ref[k + PX].T
        for f, column in enumerate((6, 1, 2, 3, 4, 5)):
            lead_ref[k, f] = jnp.broadcast_to(turned[:, column : column + 1], (128, 128))
        a1_ref[k] = jnp.zeros((3, 128, 128), F32)
        return carry

    lax.fori_loop(0, OWN, spread, 0, unroll=UNROLL)

    def one(k, carry):
        ia = k + PX
        x = k & 7
        p = (first + ia) & 127
        chunks = (fill_ref[p] + 7) // 8
        below = low_ref[0, p] // 8

        def lower(g, carry):
            c = g * GROUP
            leads = [lead_of(k, c + n) for n in range(GROUP)]
            put(k, c, plane_units(ia, x, c, leads))
            return carry

        def upper(g, carry):
            c = g * GROUP
            leads = [lead_of(k, c + n) for n in range(GROUP)]
            put(k, c, up_units(ia, x, leads, 0, plane_units(ia, x, c, leads)))
            return carry

        cut = below // GROUP
        end = (chunks + GROUP - 1) // GROUP
        lax.fori_loop(0, cut, lower, 0)
        lax.fori_loop(cut, end, upper, 0)

        @pl.when(spill)
        def _():
            def more(c, carry):
                force = [tuple(a1_ref[k, d, pl.ds(c * 8, 8), :] for d in range(3))]
                put(k, c, up_units(ia, x, [lead_of(k, c)], 24, force))
                return carry

            lax.fori_loop(below, chunks, more, 0)

        return carry

    lax.fori_loop(0, OWN, one, 0)

    def gather(k, carry):
        for d in range(3):
            own_ref[d, pl.ds(k + PX, 1), :] = jnp.sum(a1_ref[k, d].T, axis=0, keepdims=True)
        return carry

    lax.fori_loop(0, OWN, gather, 0, unroll=UNROLL)

    def fold(ref, k, d):
        return jnp.sum(ref[k, 8 * d : 8 * d + 8, :], axis=0, keepdims=True)

    def finish(p, carry):
        for d in range(3):
            own_ref[d, pl.ds(2 * p, 1), :] += fold(acc_ref, 2 * p, d)
            own_ref[d, pl.ds(2 * p + 1, 1), :] += fold(acc_ref, 2 * p + 1, d)
            a = fold(accu_ref, p, d)
            b = fold(accu_ref, 24 + p, d)
            up_ref[d, pl.ds(2 * p, 1), :] = jnp.where(half[0:1], a, pltpu.roll(b, 64, 1))
            up_ref[d, pl.ds(2 * p + 1, 1), :] = jnp.where(half[0:1], pltpu.roll(a, 64, 1), b)
        return carry

    lax.fori_loop(0, 24, finish, 0)


def kick_kernel(
    own_ref,
    up_ref,
    rank_ref,
    type_ref,
    mass_ref,
    vel_ref,
    pos_ref,
    new_vel_ref,
    new_pos_ref,
    came_ref,
    parts_ref,
    up_send,
    up_recv,
    part_send,
    part_recv,
):
    group = lax.axis_index("patch")
    groups = lax.axis_size("patch")
    below = lax.rem(group + groups - 1, groups)
    above = lax.rem(group + 1, groups)
    me = lax.axis_index("sub")
    barrier = pltpu.get_barrier_semaphore()
    pl.semaphore_signal(barrier, inc=1, device_id={"patch": below}, device_id_type=MESH)
    for step in range(1, SUBS):
        peer = lax.rem(me + step, SUBS)
        pl.semaphore_signal(barrier, inc=1, device_id={"sub": peer}, device_id_type=MESH)
    pl.semaphore_wait(barrier, SUBS)
    raised = pltpu.make_async_remote_copy(
        src_ref=up_ref,
        dst_ref=came_ref,
        send_sem=up_send,
        recv_sem=up_recv,
        device_id={"patch": above},
        device_id_type=MESH,
    )
    raised.start()
    slot = lax.broadcasted_iota(jnp.int32, (128, 128), 0).astype(F32)
    row8 = lax.broadcasted_iota(jnp.int32, (8, 128), 0)

    def unsorted(ref, k):
        hit = (rank_ref[pl.ds(k, 1), :] == slot).astype(F32).astype(BF16)
        tile = [ref[d, pl.ds(k, 1), :] for d in range(3)]
        tile = jnp.where(row8 == 0, tile[0], jnp.where(row8 == 1, tile[1], tile[2]))
        total = jnp.zeros((8, 128), F32)
        for part in split3(tile):
            total = total + jnp.dot(part, hit, preferred_element_type=F32)
        return total

    def mine(k, carry):
        total = unsorted(own_ref, k)
        for d in range(3):
            parts_ref[me, d, pl.ds(k, 1), :] = total[d : d + 1, :]
        return carry

    def theirs(k, carry):
        total = unsorted(came_ref, k)
        for d in range(3):
            parts_ref[me, d, pl.ds(k, 1), :] += total[d : d + 1, :]
        return carry

    lax.fori_loop(0, EXT, mine, 0, unroll=4)
    raised.wait()
    lax.fori_loop(0, EXT, theirs, 0, unroll=4)
    copies = []
    for step in range(1, SUBS):
        copy = pltpu.make_async_remote_copy(
            src_ref=parts_ref.at[me],
            dst_ref=parts_ref.at[me],
            send_sem=part_send.at[step - 1],
            recv_sem=part_recv.at[step - 1],
            device_id={"sub": lax.rem(me + step, SUBS)},
            device_id_type=MESH,
        )
        copy.start()
        copies.append(copy)
    kick = lookup(type_ref[...], mass_ref, KICK_SCALE, False)
    for copy in copies:
        copy.wait()
    for s in range(SUBS):
        for d in range(3):
            force = parts_ref[s, d, PX : PX + OWN, :]
            head = parts_ref[(s + SUBS - 1) % SUBS, d, PX + OWN : EXT, :]
            tail = parts_ref[(s + 1) % SUBS, d, 0:PX, :]
            force = jnp.concatenate([force[0:8] + head, force[8:24], force[24:32] + tail], axis=0)
            rows = slice(s * OWN, (s + 1) * OWN)
            velocity = vel_ref[d, rows, :] + kick[rows] * force
            new_vel_ref[d, rows, :] = velocity
            new_pos_ref[d, rows, :] = pos_ref[d, rows, :] + velocity


VM = pl.BlockSpec(memory_space=pltpu.VMEM)
SM = pl.BlockSpec(memory_space=pltpu.SMEM)


def shape(*dims, dtype=F32):
    return jax.ShapeDtypeStruct(dims, dtype)


def prep_call(positions, charges, atom_type, patch_fill, sigma_table, eps_table):
    return pl.pallas_call(
        prep_kernel,
        out_shape=(
            shape(EXT, 8, 128),
            shape(EXT, 8, 128),
            shape(EXT, 128),
            shape(8, 128, dtype=jnp.int32),
        ),
        in_specs=[VM] * 6,
        out_specs=(VM, VM, VM, VM),
        scratch_shapes=[
            pltpu.VMEM((1024, 128), F32),
            pltpu.VMEM((128, 128), F32),
            pltpu.SemaphoreType.DMA((PARTS,)),
            pltpu.SemaphoreType.DMA((PARTS,)),
        ],
        compiler_params=pltpu.CompilerParams(
            vmem_limit_bytes=VMEM_BYTES, collective_id=0, has_side_effects=True
        ),
    )(positions, charges, atom_type, patch_fill[None], sigma_table[None], eps_table[None])


def pair_call(sub, patch_fill, low, features, above):
    return pl.pallas_call(
        pair_kernel,
        out_shape=(shape(3, EXT, 128), shape(3, EXT, 128)),
        in_specs=[SM, SM, SM, VM, VM],
        out_specs=(VM, VM),
        scratch_shapes=[
            pltpu.VMEM((OWN, 6, 128, 128), F32),
            pltpu.VMEM((EXT, 8, 128), F32),
            pltpu.VMEM((OWN, 3, 128, 128), F32),
            pltpu.VMEM((EXT, 24, 128), F32),
            pltpu.VMEM((EXT, 24, 128), F32),
        ],
        compiler_params=pltpu.CompilerParams(vmem_limit_bytes=VMEM_BYTES),
    )(sub, patch_fill, low, features, above)


def kick_call(own, up, rank, atom_type, inv_mass_table, velocities, positions):
    return pl.pallas_call(
        kick_kernel,
        out_shape=(shape(3, 128, 128), shape(3, 128, 128)),
        in_specs=[VM] * 7,
        out_specs=(VM, VM),
        scratch_shapes=[
            pltpu.VMEM((3, EXT, 128), F32),
            pltpu.VMEM((SUBS, 3, EXT, 128), F32),
            pltpu.SemaphoreType.DMA,
            pltpu.SemaphoreType.DMA,
            pltpu.SemaphoreType.DMA((SUBS - 1,)),
            pltpu.SemaphoreType.DMA((SUBS - 1,)),
        ],
        compiler_params=pltpu.CompilerParams(
            vmem_limit_bytes=VMEM_BYTES, collective_id=1, has_side_effects=True
        ),
    )(own, up, rank, atom_type, inv_mass_table[None], velocities, positions)


def local(
    positions,
    velocities,
    charges,
    atom_type,
    patch_fill,
    sigma_table,
    eps_table,
    inv_mass_table,
    pair_first,
    pair_second,
):
    sub = lax.axis_index("sub").astype(jnp.int32).reshape(1)
    features, above, rank, low = prep_call(positions, charges, atom_type, patch_fill, sigma_table, eps_table)
    own, up = pair_call(sub, patch_fill, low, features, above)
    return kick_call(own, up, rank, atom_type, inv_mass_table, velocities, positions)


def solution(mesh):
    return jax.shard_map(
        local,
        mesh=mesh,
        in_specs=(
            P(None, "patch", None),
            P(None, "patch", None),
            P("patch", None),
            P("patch", None),
            P("patch"),
            P(),
            P(),
            P(),
            P("patch", "sub", None),
            P("patch", "sub", None),
        ),
        out_specs=(P(None, "patch", None), P(None, "patch", None)),
        check_vma=False,
    )
```

time: 648 us -> 74.7 us (0.12)
  starting transfers between devices: 487 us -> 0 us
  waiting for transfers between devices: 73 us -> 0 us
  Pallas kernels: 0 us -> 68.5 us
  other arithmetic: 59.3 us -> 0 us
  between operations: 14.9 us -> 0.73 us
    ppermute x6 -> x0, starting transfers between devices: 487 us -> none  [shifted(): return lax.ppermute(value, axis, pairs)]
    pallas_call x0 -> x3, Pallas kernels: none -> 68.5 us  [the longest x1 40.5 us: pair_call(): pl.pallas_call(pair_kernel, out_shape=(shape(3, EXT, 128), shape(3, EXT,...]
    psum x1 -> x0, waiting for transfers between devices: 52.4 us -> none  [local(): forces = lax.psum(gathered, 'sub')]
    reduce_sum x5 -> x0, other arithmetic: 33.8 us -> none  [the longest x4 32.7 us: pair_block(): jnp.sum(pull_x, axis=1)]
    ppermute x6 -> x0, waiting for transfers between devices: 20.6 us -> none  [shifted(): return lax.ppermute(value, axis, pairs)]
    scatter-add x8 -> x0, other arithmetic: 13.6 us -> none  [the longest x4 6.8 us: apply_block(): totals.at[:, second_local, :].add(on_second * weight_second[None, :, None])]
  transfers between devices with their start and end apart: 7 -> 0, of which waited for: 5 -> 0; matrix products, arithmetic and copies ran while one was open for 1% -> 0% of each run, Pallas kernels for 0% -> 0%
where the time goes in v1:
time: 74.7 us; the launch traced here: 74.5 us
  Pallas kernels  68.5 us (92%)
  local copies, waits for them, and re-layouts  5.26 us (7%)
    pallas_call x1, Pallas kernels, pair_call(): pl.pallas_call(pair_kernel, out_shape=(shape(3, EXT, 128), shape(3, EXT,...  40.5 us
    pallas_call x1, Pallas kernels, kick_call(): pl.pallas_call(kick_kernel, out_shape=(shape(3, 128, 128), shape(3, 128,...  14.2 us
    pallas_call x1, Pallas kernels, prep_call(): pl.pallas_call(prep_kernel, out_shape=(shape(EXT, 8, 128), shape(EXT, 8,...  13.9 us
    unnamed x22, local copies, waits for them, and re-layouts  5.26 us

profile of v1, /device:TPU:2, one launch (start us, length us, event | category | flops | bytes accessed | tf_op | source)
XLA Modules:
  0.0 74.5 jit_solution(17442473418109401092)
XLA Ops:
  0.6 0.0 copy-start.6
  0.6 0.0 copy-start.7
  0.7 0.0 copy-start.8
  0.7 0.6 copy-done.6
  1.3 0.0 copy-done.7
  1.3 0.0 copy-done.8
  1.3 0.0 copy-start
  1.3 0.9 %copy-done = f32[3,128,128]{2,1,0:T(8,128)S(1)} copy-done((f32[3,128,128]{2,1,0:T(8,128)S(1)}, f32[3,128,128]{2,1,0:T(8,128)}, u32[]{:S(2)}) %copy-start) | copy-done | bytes 196632
  2.3 0.0 copy-start.2
  2.3 0.8 %copy-done.2 = s32[128,128]{1,0:T(8,128)S(1)} copy-done((s32[128,128]{1,0:T(8,128)S(1)}, s32[128,128]{1,0:T(8,128)}, u32[]{:S(2)}) %copy-start.2) | copy-done | bytes 65560
  3.1 0.0 copy-start.5
  3.1 0.8 %copy-done.5 = f32[128,128]{1,0:T(8,128)S(1)} copy-done((f32[128,128]{1,0:T(8,128)S(1)}, f32[128,128]{1,0:T(8,128)}, u32[]{:S(2)}) %copy-start.5) | copy-done | bytes 65560
  3.9 0.0 copy-start.4
  3.9 13.9 %shard_map.95 = (f32[48,8,128]{2,1,0:T(8,128)S(1)}, f32[48,8,128]{2,1,0:T(8,128)S(1)}, f32[48,128]{1,0:T(8,128)S(1)}, s32[8,128]{1,0:T(8,128)S(1)}) custom-call(f32[3,128,128]{2,1,0:T(8,128)S(1)} %copy-done, f32[128,128]{1,0:T(8,128)S(1)} %copy-done.5, s32[128,128]{1,0:T(8,128)S(1)} %copy-done.2, s32[1,128]{1,0:T(1,128)S(1)} %bitcast.5, f32[1,8]{1,0:T(1,128)S(1)} %bitcast.6, ...), custom_call_target="tpu_custom_call" | custom-call | tf_op jit(solution)/shard_map/pallas_call | solution.py:406
  17.8 0.0 copy-start.1
  17.8 0.0 copy-start.3
  17.8 40.5 %shard_map.96 = (f32[3,48,128]{2,1,0:T(8,128)S(1)}, f32[3,48,128]{2,1,0:T(8,128)S(1)}) custom-call(s32[1]{0:T(128)} %bitcast.sub_ref, s32[128]{0:T(128)S(1)} %copy-done.6, s32[8,128]{1,0:T(8,128)S(1)} %get-tuple-element.8.low_ref, f32[48,8,128]{2,1,0:T(8,128)S(1)} %get-tuple-element.9.fj_ref, f32[48,8,128]{2,1,0:T(8,128)S(1)} %get-tuple-element.10.fu_ref), custom_call_target="tpu_custom_call" | custom-call | tf_op jit(solution)/shard_map/pallas_call | solution.py:429
  58.3 0.0 copy-start.9
  58.3 0.0 copy-done.4
  58.4 0.0 copy-done.1
  58.4 0.0 copy-done.3
  58.4 0.6 copy-done.9
  59.0 14.2 %shard_map.97 = (f32[3,128,128]{2,1,0:T(8,128)S(1)}, f32[3,128,128]{2,1,0:T(8,128)S(1)}) custom-call(f32[3,48,128]{2,1,0:T(8,128)S(1)} %get-tuple-element.11.own_ref, f32[3,48,128]{2,1,0:T(8,128)S(1)} %get-tuple-element.12.up_ref, f32[48,128]{1,0:T(8,128)S(1)} %get-tuple-element.13.rank_ref, s32[128,128]{1,0:T(8,128)S(1)} %copy-done.3, f32[1,8]{1,0:T(1,128)S(1)} %bitcast.8, ...), custom_call_target="tpu_custom_call" | custom-call | tf_op jit(solution)/shard_map/pallas_call | solution.py:446
  73.2 0.7 copy.12
  73.9 0.7 copy.13
Async XLA Ops:
  0.6 0.7 copy-start.6
  0.6 0.7 copy-start.7
  0.7 0.7 copy-start.8
  1.3 0.9 %copy-start = (f32[3,128,128]{2,1,0:T(8,128)S(1)}, f32[3,128,128]{2,1,0:T(8,128)}, u32[]{:S(2)}) copy-start(f32[3,128,128]{2,1,0:T(8,128)} %pos_ref.3) | copy-start | bytes 589828
  2.3 0.8 %copy-start.2 = (s32[128,128]{1,0:T(8,128)S(1)}, s32[128,128]{1,0:T(8,128)}, u32[]{:S(2)}) copy-start(s32[128,128]{1,0:T(8,128)} %type_ref.3) | copy-start | bytes 196612
  3.1 0.8 %copy-start.5 = (f32[128,128]{1,0:T(8,128)S(1)}, f32[128,128]{1,0:T(8,128)}, u32[]{:S(2)}) copy-start(f32[128,128]{1,0:T(8,128)} %charge_ref.1) | copy-start | bytes 196612
  3.9 54.4 %copy-start.4 = (f32[3,128,128]{2,1,0:T(8,128)S(1)}, f32[3,128,128]{2,1,0:T(8,128)}, u32[]{:S(2)}) copy-start(f32[3,128,128]{2,1,0:T(8,128)} %vel_ref.1) | copy-start | bytes 589828
  17.8 40.6 %copy-start.1 = (f32[3,128,128]{2,1,0:T(8,128)S(1)}, f32[3,128,128]{2,1,0:T(8,128)}, u32[]{:S(2)}) copy-start(f32[3,128,128]{2,1,0:T(8,128)} %pos_ref.3) | copy-start | bytes 589828
  17.8 40.6 %copy-start.3 = (s32[128,128]{1,0:T(8,128)S(1)}, s32[128,128]{1,0:T(8,128)}, u32[]{:S(2)}) copy-start(s32[128,128]{1,0:T(8,128)} %type_ref.3) | copy-start | bytes 196612
  58.3 0.7 copy-start.9

commit v2 on v1

v2 whole, which is shorter than its diff:
```python
import math

import jax
import jax.numpy as jnp
from jax import lax
from jax.experimental import pallas as pl
from jax.experimental.pallas import tpu as pltpu
from jax.sharding import PartitionSpec as P

PX = 8
EXT = 48
OWN = 32
SUBS = 4
VMEM_BYTES = 48 * 1024 * 1024
COULOMB = 332.0636
SPLIT_BETA = 0.2
CUTOFF_SQ = 144.0
KICK_SCALE = 0.04
CELL_WIDTH = 12.0
CELL_HEIGHT = 24.0
STEP_W = SPLIT_BETA * CELL_WIDTH
STEP_H = SPLIT_BETA * CELL_HEIGHT
CUT = SPLIT_BETA * SPLIT_BETA * CUTOFF_SQ
GAUSS = 2.0 / math.sqrt(math.pi)
LOG2E = math.log2(math.e)
SIGMA_SCALE = SPLIT_BETA * 0.5 * 2.0 ** (1.0 / 6.0)
DEPTH_SCALE = math.sqrt(12.0 * SPLIT_BETA)
CHARGE_SCALE = math.sqrt(COULOMB * SPLIT_BETA * SPLIT_BETA)
FAR = 1.0e4
FIRST = 16
SECOND = 24
MESH = pl.DeviceIdType.MESH
F32 = jnp.float32
BF16 = jnp.bfloat16


def stacked(tile):
    high = tile.astype(BF16).astype(F32)
    rest = tile - high
    mid = rest.astype(BF16).astype(F32)
    return jnp.concatenate([high, mid, rest - mid, jnp.zeros((8, 128), F32)], axis=0).astype(BF16)


def lookup(kind, table_ref, scale, root):
    value = jnp.zeros(kind.shape, F32)
    for t in range(8):
        value = jnp.where(kind == t, table_ref[0:1, t : t + 1], value)
    if root:
        value = jnp.sqrt(value)
    return value * scale


def first_kernel(
    pos_ref,
    charge_ref,
    type_ref,
    fill_ref,
    sigma_ref,
    eps_ref,
    fj_ref,
    fu_ref,
    rank_ref,
    own_ref,
    feat_ref,
    place_ref,
    lead0_ref,
    lead1_ref,
    sum0_ref,
    sum1_ref,
    acc_ref,
    send_sem,
    recv_sem,
):
    group = lax.axis_index("patch")
    groups = lax.axis_size("patch")
    below = lax.rem(group + groups - 1, groups)
    above = lax.rem(group + 1, groups)
    barrier = pltpu.get_barrier_semaphore()
    pl.semaphore_signal(barrier, inc=1, device_id={"patch": above}, device_id_type=MESH)
    lane = lax.broadcasted_iota(jnp.int32, (128, 128), 1)
    row = lax.broadcasted_iota(jnp.int32, (128, 128), 0)
    fill = jnp.broadcast_to(fill_ref[0:1, :].astype(F32), (128, 128)).T
    present = lane.astype(F32) < fill
    kind = type_ref[...]
    z = pos_ref[2]
    feat_ref[0:128] = jnp.where(present, pos_ref[0] * SPLIT_BETA, -FAR)
    feat_ref[128:256] = pos_ref[1] * SPLIT_BETA
    feat_ref[256:384] = z * SPLIT_BETA
    feat_ref[384:512] = jnp.where(present, charge_ref[...] * CHARGE_SCALE, 0.0)
    feat_ref[512:640] = lookup(kind, sigma_ref, SIGMA_SCALE, False)
    feat_ref[640:768] = jnp.where(present, lookup(kind, eps_ref, DEPTH_SCALE, True), 0.0)
    feat_ref[768:896] = kind.astype(F32)
    low = jnp.logical_and(present, z < 0.5 * CELL_HEIGHT).astype(F32)
    high = jnp.logical_and(present, z >= 0.5 * CELL_HEIGHT).astype(F32)
    upto = (row <= lane).astype(F32).astype(BF16)
    low_upto = jnp.dot(low.astype(BF16), upto, preferred_element_type=F32)
    high_upto = jnp.dot(high.astype(BF16), upto, preferred_element_type=F32)
    low_count = jnp.sum(low, axis=1, keepdims=True)
    high_count = jnp.sum(high, axis=1, keepdims=True)
    fits = jnp.logical_and(low_count <= 64.0, high_count <= 64.0)
    column = lane.astype(F32)
    gap = low_count + column - fill
    place_ref[...] = jnp.where(
        low > 0.0,
        low_upto - 1.0,
        jnp.where(
            high > 0.0,
            jnp.where(fits, 64.0, low_count) + high_upto - 1.0,
            jnp.where(jnp.logical_and(fits, gap < 64.0), gap, column),
        ),
    )
    feat_ref[896:1024] = jnp.broadcast_to(jnp.where(fits, 0.0, 1.0), (128, 128))
    first = lax.axis_index("sub") * OWN - PX + 128
    slot = row.astype(F32)

    def one(k, carry):
        p = (first + k) & 127
        place = place_ref[pl.ds(p, 1), :]
        rank_ref[pl.ds(k, 1), :] = place
        hit = (place == slot).astype(F32).astype(BF16)
        tile = feat_ref[pl.ds(p, 8, stride=128), :]
        total = lax.dot_general(stacked(tile), hit, (((1,), (1,)), ((), ())), preferred_element_type=F32)
        fj_ref[k] = total[0:8] + total[8:16] + total[16:24]
        return carry

    lax.fori_loop(0, EXT, one, 0, unroll=4)
    clear(acc_ref, own_ref)
    pl.semaphore_wait(barrier, 1)
    copy = pltpu.make_async_remote_copy(
        src_ref=fj_ref,
        dst_ref=fu_ref,
        send_sem=send_sem,
        recv_sem=recv_sem,
        device_id={"patch": below},
        device_id_type=MESH,
    )
    copy.start()
    plane_patches(0, FIRST, fj_ref, (lead0_ref, lead1_ref), (sum0_ref, sum1_ref), acc_ref, own_ref)
    add_folded(acc_ref, own_ref)
    copy.wait()


def spread(tile, lead_ref, rows):
    row8 = lax.broadcasted_iota(jnp.int32, (8, 128), 0)
    hidden = jnp.logical_and(row8 == 0, tile < -1.0)
    turned = jnp.where(hidden, FAR, tile).T
    for f in range(6):
        lead_ref[f] = jnp.broadcast_to(turned[128 - rows : 128, f : f + 1], (rows, 128))


def pair_block(lead_ref, cols, same):
    rows = lead_ref.shape[1]
    delta = [lead_ref[d] - cols[d : d + 1] for d in range(3)]
    v = delta[0] * delta[0] + delta[1] * delta[1] + delta[2] * delta[2]
    w = lax.rsqrt(v)
    w2 = w * w
    u = (lead_ref[4] + cols[4:5]) * w
    u = u * u
    u = u * u * u
    screened = (1.0 - lax.erf(v * w)) * w + GAUSS * jnp.exp2(v * (-LOG2E))
    both = (lead_ref[5] * cols[5:6]) * (u * u - u) + (lead_ref[3] * cols[3:4]) * screened
    keep = v < CUT
    if same:
        i = lax.broadcasted_iota(jnp.int32, (rows, 128), 0)
        j = lax.broadcasted_iota(jnp.int32, (rows, 128), 1)
        keep = jnp.logical_and(keep, i != j)
    force = jnp.where(keep, both * w2, 0.0)
    return [force * t for t in delta]


def fold8(value):
    total = value[0:8]
    for r in range(8, value.shape[0], 8):
        total = total + value[r : r + 8]
    return total


def moved(tile, x, y, z):
    row8 = lax.broadcasted_iota(jnp.int32, (8, 128), 0)
    return tile + jnp.where(row8 == 0, x, jnp.where(row8 == 1, y, jnp.where(row8 == 2, z, 0.0)))


def plane_patch(k, fj_ref, lead_ref, sum_ref, acc_ref):
    ia = k + PX
    x = k % PX
    left = ia - x + (x + PX - 1) % PX
    right = ia - x + (x + 1) % PX
    kinds = ((0, 0, ia), (1, 0, right), (-1, 1, left + PX), (0, 1, ia + PX), (1, 1, right + PX))
    for n, (sx, sy, b) in enumerate(kinds):
        pull = pair_block(lead_ref, moved(fj_ref[b], STEP_W * sx, STEP_W * sy, 0.0), n == 0)
        for d in range(3):
            if n == 0:
                sum_ref[d] = pull[d]
            else:
                sum_ref[d] += pull[d]
                acc_ref[b, 8 * d : 8 * d + 8, :] -= fold8(pull[d])


def plane_patches(start, stop, fj_ref, leads, sums, acc_ref, own_ref):
    def two(t, carry):
        k = start + 2 * t
        for n in range(2):
            plane_patch(k + n, fj_ref, leads[n], sums[n], acc_ref)
            spread(fj_ref[k + n + 2 + PX], leads[n], 128)
            for d in range(3):
                own_ref[d, pl.ds(k + n + PX, 1), :] = jnp.sum(sums[n][d].T, axis=0, keepdims=True)
        return carry

    spread(fj_ref[start + PX], leads[0], 128)
    spread(fj_ref[start + 1 + PX], leads[1], 128)
    lax.fori_loop(0, (stop - start) // 2, two, 0)


def clear(acc_ref, own_ref):
    def one(k, carry):
        acc_ref[k] = jnp.zeros((24, 128), F32)
        return carry

    lax.fori_loop(0, EXT, one, 0, unroll=4)
    own_ref[...] = jnp.zeros(own_ref.shape, F32)


def fold(ref, k, d):
    return jnp.sum(ref[k, 8 * d : 8 * d + 8, :], axis=0, keepdims=True)


def add_folded(acc_ref, own_ref):
    def one(k, carry):
        for d in range(3):
            own_ref[d, pl.ds(k, 1), :] += fold(acc_ref, k, d)
        return carry

    lax.fori_loop(PX, EXT, one, 0, unroll=4)


def up_kernel(
    fj_ref, fu_ref, up_ref, own_ref, turn_ref, lead0_ref, lead1_ref, sum0_ref, sum1_ref, acc_ref, accr_ref, full_ref, sumf_ref
):
    lane8 = lax.broadcasted_iota(jnp.int32, (8, 128), 1)
    row8 = lax.broadcasted_iota(jnp.int32, (8, 128), 0)
    half = lane8 < 64
    leads = (lead0_ref, lead1_ref)
    sums = (sum0_ref, sum1_ref)
    sides = [(dr, dx) for dr in (-1, 0, 1) for dx in (-1, 0, 1)]

    def start(p, worst):
        tile = fu_ref[p]
        turn_ref[p] = pltpu.roll(tile, 64, 1)
        acc_ref[p] = jnp.zeros((24, 128), F32)
        accr_ref[p] = jnp.zeros((24, 128), F32)
        return jnp.maximum(worst, jnp.maximum(tile[7:8], fj_ref[p, 7:8, :]))

    worst = lax.fori_loop(0, EXT, start, jnp.zeros((1, 128), F32), unroll=4)
    spill = jnp.max(worst) > 0.0

    def others(k):
        x = k % PX
        base = k + PX - x
        return [(base + PX * dr + (x + dx + PX) % PX, STEP_W * dx, STEP_W * dr) for dr, dx in sides]

    def finish(k, sum_ref, rows):
        for d in range(3):
            total = jnp.sum(sum_ref[d].T, axis=0, keepdims=True)
            if rows < 128:
                total = jnp.concatenate([jnp.zeros((1, 128 - rows), F32), total], axis=1)
            own_ref[d, pl.ds(k, 1), :] = total

    @pl.when(jnp.logical_not(spill))
    def _():
        def patch(k, lead_ref, sum_ref):
            near = others(k)
            for n in range(0, 9, 2):
                p, px, py = near[n]
                cols = moved(fu_ref[p], px, py, STEP_H)
                if n < 8:
                    r, rx, ry = near[n + 1]
                    cols = jnp.where(half, cols, moved(turn_ref[r], rx, ry, STEP_H))
                else:
                    cols = jnp.where(jnp.logical_or(half, row8 > 0), cols, -FAR)
                pull = pair_block(lead_ref, cols, False)
                for d in range(3):
                    if n == 0:
                        sum_ref[d] = pull[d]
                    else:
                        sum_ref[d] += pull[d]
                    back = fold8(pull[d])
                    acc_ref[p, 8 * d : 8 * d + 8, :] -= back
                    if n < 8:
                        accr_ref[r, 8 * d : 8 * d + 8, :] -= back

        def two(t, carry):
            k = 2 * t
            for n in range(2):
                patch(k + n, leads[n], sums[n])
                spread(fj_ref[k + n + 2 + PX], leads[n], 64)
                finish(k + n, sums[n], 64)
            return carry

        spread(fj_ref[PX], leads[0], 64)
        spread(fj_ref[PX + 1], leads[1], 64)
        lax.fori_loop(0, OWN // 2, two, 0)

    @pl.when(spill)
    def _():
        def one(k, carry):
            spread(fj_ref[k + PX], full_ref, 128)
            for n, (p, px, py) in enumerate(others(k)):
                pull = pair_block(full_ref, moved(fu_ref[p], px, py, STEP_H), False)
                for d in range(3):
                    if n == 0:
                        sumf_ref[d] = pull[d]
                    else:
                        sumf_ref[d] += pull[d]
                    acc_ref[p, 8 * d : 8 * d + 8, :] -= fold8(pull[d])
            finish(k, sumf_ref, 128)
            return carry

        lax.fori_loop(0, OWN, one, 0)

    @pl.when(jnp.logical_not(spill))
    def _():
        def one(p, carry):
            for d in range(3):
                total = fold(acc_ref, p, d) + pltpu.roll(fold(accr_ref, p, d), 64, 1)
                up_ref[d, pl.ds(p, 1), :] = jnp.where(half[0:1], total, 0.0)
            return carry

        lax.fori_loop(0, EXT, one, 0, unroll=4)

    @pl.when(spill)
    def _():
        def one(p, carry):
            for d in range(3):
                up_ref[d, pl.ds(p, 1), :] = fold(acc_ref, p, d)
            return carry

        lax.fori_loop(0, EXT, one, 0)


def kick_kernel(
    fj_ref,
    first_ref,
    rise_ref,
    up_ref,
    rank_ref,
    type_ref,
    mass_ref,
    vel_ref,
    pos_ref,
    new_vel_ref,
    new_pos_ref,
    own_ref,
    lead0_ref,
    lead1_ref,
    sum0_ref,
    sum1_ref,
    acc_ref,
    came_ref,
    parts_ref,
    up_send,
    up_recv,
    part_send,
    part_recv,
):
    group = lax.axis_index("patch")
    groups = lax.axis_size("patch")
    below = lax.rem(group + groups - 1, groups)
    above = lax.rem(group + 1, groups)
    me = lax.axis_index("sub")
    barrier = pltpu.get_barrier_semaphore()
    pl.semaphore_signal(barrier, inc=1, device_id={"patch": below}, device_id_type=MESH)
    for step in range(1, SUBS):
        peer = lax.rem(me + step, SUBS)
        pl.semaphore_signal(barrier, inc=1, device_id={"sub": peer}, device_id_type=MESH)
    clear(acc_ref, own_ref)
    work = (fj_ref, (lead0_ref, lead1_ref), (sum0_ref, sum1_ref), acc_ref, own_ref)
    plane_patches(FIRST, SECOND, *work)
    pl.semaphore_wait(barrier, SUBS)
    raised = pltpu.make_async_remote_copy(
        src_ref=up_ref,
        dst_ref=came_ref,
        send_sem=up_send,
        recv_sem=up_recv,
        device_id={"patch": above},
        device_id_type=MESH,
    )
    raised.start()
    plane_patches(SECOND, OWN, *work)
    add_folded(acc_ref, own_ref)
    for d in range(3):
        own_ref[d] += first_ref[d]
        own_ref[d, PX : PX + OWN, :] += rise_ref[d]
    slot = lax.broadcasted_iota(jnp.int32, (128, 128), 0).astype(F32)
    row8 = lax.broadcasted_iota(jnp.int32, (8, 128), 0)
    raised.wait()

    def unsort(k, carry):
        hit = (rank_ref[pl.ds(k, 1), :] == slot).astype(F32).astype(BF16)
        tile = [own_ref[d, pl.ds(k, 1), :] + came_ref[d, pl.ds(k, 1), :] for d in range(3)]
        tile = jnp.where(row8 == 0, tile[0], jnp.where(row8 == 1, tile[1], tile[2]))
        total = jnp.dot(stacked(tile), hit, preferred_element_type=F32)
        total = total[0:8] + total[8:16] + total[16:24]
        for d in range(3):
            parts_ref[me, d, pl.ds(k, 1), :] = total[d : d + 1, :]
        return carry

    lax.fori_loop(0, EXT, unsort, 0, unroll=4)
    copies = []
    for step in range(1, SUBS):
        copy = pltpu.make_async_remote_copy(
            src_ref=parts_ref.at[me],
            dst_ref=parts_ref.at[me],
            send_sem=part_send.at[step - 1],
            recv_sem=part_recv.at[step - 1],
            device_id={"sub": lax.rem(me + step, SUBS)},
            device_id_type=MESH,
        )
        copy.start()
        copies.append(copy)
    kick = lookup(type_ref[...], mass_ref, KICK_SCALE, False)
    for copy in copies:
        copy.wait()
    for s in range(SUBS):
        for d in range(3):
            force = parts_ref[s, d, PX : PX + OWN, :]
            head = parts_ref[(s + SUBS - 1) % SUBS, d, PX + OWN : EXT, :]
            tail = parts_ref[(s + 1) % SUBS, d, 0:PX, :]
            force = jnp.concatenate([force[0:8] + head, force[8:24], force[24:32] + tail], axis=0)
            rows = slice(s * OWN, (s + 1) * OWN)
            velocity = vel_ref[d, rows, :] + kick[rows] * force
            new_vel_ref[d, rows, :] = velocity
            new_pos_ref[d, rows, :] = pos_ref[d, rows, :] + velocity


VM = pl.BlockSpec(memory_space=pltpu.VMEM)


def shape(*dims, dtype=F32):
    return jax.ShapeDtypeStruct(dims, dtype)


def work_shapes(rows):
    lead = pltpu.VMEM((6, rows, 128), F32)
    total = pltpu.VMEM((3, rows, 128), F32)
    return [lead, lead, total, total, pltpu.VMEM((EXT, 24, 128), F32)]


def first_call(positions, charges, atom_type, patch_fill, sigma_table, eps_table):
    return pl.pallas_call(
        first_kernel,
        out_shape=(shape(EXT, 8, 128), shape(EXT, 8, 128), shape(EXT, 128), shape(3, EXT, 128)),
        in_specs=[VM] * 6,
        out_specs=(VM, VM, VM, VM),
        scratch_shapes=[pltpu.VMEM((1024, 128), F32), pltpu.VMEM((128, 128), F32)]
        + work_shapes(128)
        + [pltpu.SemaphoreType.DMA, pltpu.SemaphoreType.DMA],
        compiler_params=pltpu.CompilerParams(
            vmem_limit_bytes=VMEM_BYTES, collective_id=0, has_side_effects=True
        ),
    )(positions, charges, atom_type, patch_fill[None], sigma_table[None], eps_table[None])


def up_call(features, above):
    return pl.pallas_call(
        up_kernel,
        out_shape=(shape(3, EXT, 128), shape(3, OWN, 128)),
        in_specs=[VM] * 2,
        out_specs=(VM, VM),
        scratch_shapes=[pltpu.VMEM((EXT, 8, 128), F32)]
        + work_shapes(64)
        + [pltpu.VMEM((EXT, 24, 128), F32), pltpu.VMEM((6, 128, 128), F32), pltpu.VMEM((3, 128, 128), F32)],
        compiler_params=pltpu.CompilerParams(vmem_limit_bytes=VMEM_BYTES),
    )(features, above)


def kick_call(features, first, rise, up, rank, atom_type, inv_mass_table, velocities, positions):
    return pl.pallas_call(
        kick_kernel,
        out_shape=(shape(3, 128, 128), shape(3, 128, 128)),
        in_specs=[VM] * 9,
        out_specs=(VM, VM),
        scratch_shapes=[pltpu.VMEM((3, EXT, 128), F32)]
        + work_shapes(128)
        + [
            pltpu.VMEM((3, EXT, 128), F32),
            pltpu.VMEM((SUBS, 3, EXT, 128), F32),
            pltpu.SemaphoreType.DMA,
            pltpu.SemaphoreType.DMA,
            pltpu.SemaphoreType.DMA((SUBS - 1,)),
            pltpu.SemaphoreType.DMA((SUBS - 1,)),
        ],
        compiler_params=pltpu.CompilerParams(
            vmem_limit_bytes=VMEM_BYTES, collective_id=1, has_side_effects=True
        ),
    )(features, first, rise, up, rank, atom_type, inv_mass_table[None], velocities, positions)


def local(
    positions,
    velocities,
    charges,
    atom_type,
    patch_fill,
    sigma_table,
    eps_table,
    inv_mass_table,
    pair_first,
    pair_second,
):
    features, above, rank, first = first_call(
        positions, charges, atom_type, patch_fill, sigma_table, eps_table
    )
    up, rise = up_call(features, above)
    return kick_call(features, first, rise, up, rank, atom_type, inv_mass_table, velocities, positions)


def solution(mesh):
    return jax.shard_map(
        local,
        mesh=mesh,
        in_specs=(
            P(None, "patch", None),
            P(None, "patch", None),
            P("patch", None),
            P("patch", None),
            P("patch"),
            P(),
            P(),
            P(),
            P("patch", "sub", None),
            P("patch", "sub", None),
        ),
        out_specs=(P(None, "patch", None), P(None, "patch", None)),
        check_vma=False,
    )
```

time: 74.7 us -> 54.3 us (0.73)
  Pallas kernels: 68.5 us -> 48.1 us
    pallas_call x2, Pallas kernels: 54.4 us -> 31.9 us  [the longest x1 17.3 us: first_call(): pl.pallas_call(first_kernel, out_shape=(shape(EXT, 8, 128), shape(EXT, 8,...]
    pallas_call x1, Pallas kernels: 14.2 us -> 16.1 us  [kick_call(): pl.pallas_call(kick_kernel, out_shape=(shape(3, 128, 128), shape(3, 128,...]
where the time goes in v2:
time: 54.3 us; the launch traced here: 54 us
  Pallas kernels  48.1 us (89%)
  local copies, waits for them, and re-layouts  5.26 us (10%)
  between operations  0.73 us (1%)
    pallas_call x1, Pallas kernels, first_call(): pl.pallas_call(first_kernel, out_shape=(shape(EXT, 8, 128), shape(EXT, 8,...  17.3 us
    pallas_call x1, Pallas kernels, kick_call(): pl.pallas_call(kick_kernel, out_shape=(shape(3, 128, 128), shape(3, 128,...  16.1 us
    pallas_call x1, Pallas kernels, up_call(): pl.pallas_call(up_kernel, out_shape=(shape(3, EXT, 128), shape(3, OWN, 12...  14.7 us
    unnamed x22, local copies, waits for them, and re-layouts  5.26 us

profile of v2, /device:TPU:2, one launch (start us, length us, event | category | flops | bytes accessed | tf_op | source)
XLA Modules:
  0.0 54.0 jit_solution(9647635208502917333)
XLA Ops:
  0.6 0.0 copy-start.6
  0.6 0.0 copy-start.7
  0.7 0.0 copy-start.8
  0.7 0.6 %copy-done.6 = s32[128]{0:T(128)S(1)} copy-done((s32[128]{0:T(128)S(1)}, s32[128]{0:T(128)}, u32[]{:S(2)}) %copy-start.6) | copy-done | bytes 536
  1.3 0.0 copy-done.7
  1.3 0.0 copy-done.8
  1.3 0.0 copy-start
  1.3 0.9 %copy-done = f32[3,128,128]{2,1,0:T(8,128)S(1)} copy-done((f32[3,128,128]{2,1,0:T(8,128)S(1)}, f32[3,128,128]{2,1,0:T(8,128)}, u32[]{:S(2)}) %copy-start) | copy-done | bytes 196632
  2.2 0.0 copy-start.2
  2.2 0.8 %copy-done.2 = s32[128,128]{1,0:T(8,128)S(1)} copy-done((s32[128,128]{1,0:T(8,128)S(1)}, s32[128,128]{1,0:T(8,128)}, u32[]{:S(2)}) %copy-start.2) | copy-done | bytes 65560
  3.1 0.0 copy-start.5
  3.1 0.8 %copy-done.5 = f32[128,128]{1,0:T(8,128)S(1)} copy-done((f32[128,128]{1,0:T(8,128)S(1)}, f32[128,128]{1,0:T(8,128)}, u32[]{:S(2)}) %copy-start.5) | copy-done | bytes 65560
  3.9 0.0 copy-start.4
  3.9 17.3 %shard_map.95 = (f32[48,8,128]{2,1,0:T(8,128)S(1)}, f32[48,8,128]{2,1,0:T(8,128)S(1)}, f32[48,128]{1,0:T(8,128)S(1)}, f32[3,48,128]{2,1,0:T(8,128)S(1)}) custom-call(f32[3,128,128]{2,1,0:T(8,128)S(1)} %copy-done, f32[128,128]{1,0:T(8,128)S(1)} %copy-done.5, s32[128,128]{1,0:T(8,128)S(1)} %copy-done.2, s32[1,128]{1,0:T(1,128)S(1)} %bitcast.4, ...), custom_call_target="tpu_custom_call" | custom-call | tf_op jit(solution)/shard_map/pallas_call | solution.py:449
  21.2 0.0 copy-start.1
  21.2 0.0 copy-start.3
  21.2 14.7 %shard_map.96 = (f32[3,48,128]{2,1,0:T(8,128)S(1)}, f32[3,32,128]{2,1,0:T(8,128)S(1)}) custom-call(f32[48,8,128]{2,1,0:T(8,128)S(1)} %get-tuple-element.8.fj_ref, f32[48,8,128]{2,1,0:T(8,128)S(1)} %get-tuple-element.10.fu_ref), custom_call_target="tpu_custom_call" | custom-call | tf_op jit(solution)/shard_map/pallas_call | solution.py:464
  35.9 0.0 copy-start.9
  35.9 0.0 copy-done.4
  35.9 0.0 copy-done.1
  35.9 0.0 copy-done.3
  35.9 0.6 %copy-done.9 = f32[8]{0:T(128)S(1)} copy-done((f32[8]{0:T(128)S(1)}, f32[8]{0:T(128)}, u32[]{:S(2)}) %copy-start.9) | copy-done | bytes 56
  36.6 16.1 %shard_map.97 = (f32[3,128,128]{2,1,0:T(8,128)S(1)}, f32[3,128,128]{2,1,0:T(8,128)S(1)}) custom-call(f32[48,8,128]{2,1,0:T(8,128)S(1)} %get-tuple-element.8.fj_ref, f32[3,48,128]{2,1,0:T(8,128)S(1)} %get-tuple-element.9.first_ref, f32[3,32,128]{2,1,0:T(8,128)S(1)} %get-tuple-element.11.rise_ref, f32[3,48,128]{2,1,0:T(8,128)S(1)} %get-tuple-element.12.up_ref, ...), custom_call_target="tpu_custom_call" | custom-call | tf_op jit(solution)/shard_map/pallas_call | solution.py:477
  52.7 0.7 %copy.12 = f32[3,128,128]{2,1,0:T(8,128)} copy(f32[3,128,128]{2,1,0:T(8,128)S(1)} %get-tuple-element.16) | data formatting | bytes 393216
  53.4 0.7 %copy.13 = f32[3,128,128]{2,1,0:T(8,128)} copy(f32[3,128,128]{2,1,0:T(8,128)S(1)} %get-tuple-element.17) | data formatting | bytes 393216
Async XLA Ops:
  0.6 0.7 %copy-start.6 = (s32[128]{0:T(128)S(1)}, s32[128]{0:T(128)}, u32[]{:S(2)}) copy-start(s32[128]{0:T(128)} %param.14) | copy-start | bytes 1540
  0.6 0.7 %copy-start.7 = (f32[8]{0:T(128)S(1)}, f32[8]{0:T(128)}, u32[]{:S(2)}) copy-start(f32[8]{0:T(128)} %param.15) | copy-start | bytes 100
  0.7 0.7 %copy-start.8 = (f32[8]{0:T(128)S(1)}, f32[8]{0:T(128)}, u32[]{:S(2)}) copy-start(f32[8]{0:T(128)} %param.16) | copy-start | bytes 100
  1.3 0.9 %copy-start = (f32[3,128,128]{2,1,0:T(8,128)S(1)}, f32[3,128,128]{2,1,0:T(8,128)}, u32[]{:S(2)}) copy-start(f32[3,128,128]{2,1,0:T(8,128)} %pos_ref.3) | copy-start | bytes 589828
  2.2 0.8 %copy-start.2 = (s32[128,128]{1,0:T(8,128)S(1)}, s32[128,128]{1,0:T(8,128)}, u32[]{:S(2)}) copy-start(s32[128,128]{1,0:T(8,128)} %type_ref.3) | copy-start | bytes 196612
  3.1 0.8 %copy-start.5 = (f32[128,128]{1,0:T(8,128)S(1)}, f32[128,128]{1,0:T(8,128)}, u32[]{:S(2)}) copy-start(f32[128,128]{1,0:T(8,128)} %charge_ref.1) | copy-start | bytes 196612
  3.9 32.0 %copy-start.4 = (f32[3,128,128]{2,1,0:T(8,128)S(1)}, f32[3,128,128]{2,1,0:T(8,128)}, u32[]{:S(2)}) copy-start(f32[3,128,128]{2,1,0:T(8,128)} %vel_ref.1) | copy-start | bytes 589828
  21.2 14.7 %copy-start.1 = (f32[3,128,128]{2,1,0:T(8,128)S(1)}, f32[3,128,128]{2,1,0:T(8,128)}, u32[]{:S(2)}) copy-start(f32[3,128,128]{2,1,0:T(8,128)} %pos_ref.3) | copy-start | bytes 589828
  21.2 14.7 %copy-start.3 = (s32[128,128]{1,0:T(8,128)S(1)}, s32[128,128]{1,0:T(8,128)}, u32[]{:S(2)}) copy-start(s32[128,128]{1,0:T(8,128)} %type_ref.3) | copy-start | bytes 196612
  35.9 0.7 %copy-start.9 = (f32[8]{0:T(128)S(1)}, f32[8]{0:T(128)}, u32[]{:S(2)}) copy-start(f32[8]{0:T(128)} %param.17) | copy-start | bytes 100

commit v3 on v2

--- a/solution.py
+++ b/solution.py
@@ -27,8 +27,10 @@
 DEPTH_SCALE = math.sqrt(12.0 * SPLIT_BETA)
 CHARGE_SCALE = math.sqrt(COULOMB * SPLIT_BETA * SPLIT_BETA)
 FAR = 1.0e4
-FIRST = 16
-SECOND = 24
+FIRST = 4
+SECOND = 12
+THIRD = 20
+PIECES = 2
 MESH = pl.DeviceIdType.MESH
 F32 = jnp.float32
 BF16 = jnp.bfloat16
@@ -51,16 +53,16 @@
 
 
 def first_kernel(
-    pos_ref,
-    charge_ref,
-    type_ref,
-    fill_ref,
-    sigma_ref,
-    eps_ref,
+    atom_hbm,
+    fill_hbm,
+    sigma_hbm,
+    eps_hbm,
+    mass_hbm,
     fj_ref,
     fu_ref,
     rank_ref,
     own_ref,
+    kick_ref,
     feat_ref,
     place_ref,
     lead0_ref,
@@ -68,28 +70,51 @@
     sum0_ref,
     sum1_ref,
     acc_ref,
+    atom_ref,
+    fill_ref,
+    sigma_ref,
+    eps_ref,
+    mass_ref,
+    load_sem,
     send_sem,
     recv_sem,
 ):
+    loads = [
+        pltpu.make_async_copy(source, target, load_sem.at[n])
+        for n, (source, target) in enumerate(
+            (
+                (atom_hbm, atom_ref),
+                (fill_hbm, fill_ref),
+                (sigma_hbm, sigma_ref),
+                (eps_hbm, eps_ref),
+                (mass_hbm, mass_ref),
+            )
+        )
+    ]
+    for load in loads:
+        load.start()
     group = lax.axis_index("patch")
     groups = lax.axis_size("patch")
     below = lax.rem(group + groups - 1, groups)
     above = lax.rem(group + 1, groups)
     barrier = pltpu.get_barrier_semaphore()
     pl.semaphore_signal(barrier, inc=1, device_id={"patch": above}, device_id_type=MESH)
+    for load in loads:
+        load.wait()
     lane = lax.broadcasted_iota(jnp.int32, (128, 128), 1)
     row = lax.broadcasted_iota(jnp.int32, (128, 128), 0)
     fill = jnp.broadcast_to(fill_ref[0:1, :].astype(F32), (128, 128)).T
     present = lane.astype(F32) < fill
-    kind = type_ref[...]
-    z = pos_ref[2]
-    feat_ref[0:128] = jnp.where(present, pos_ref[0] * SPLIT_BETA, -FAR)
-    feat_ref[128:256] = pos_ref[1] * SPLIT_BETA
+    kind = atom_ref[4]
+    z = atom_ref[2]
+    feat_ref[0:128] = jnp.where(present, atom_ref[0] * SPLIT_BETA, -FAR)
+    feat_ref[128:256] = atom_ref[1] * SPLIT_BETA
     feat_ref[256:384] = z * SPLIT_BETA
-    feat_ref[384:512] = jnp.where(present, charge_ref[...] * CHARGE_SCALE, 0.0)
+    feat_ref[384:512] = jnp.where(present, atom_ref[3] * CHARGE_SCALE, 0.0)
     feat_ref[512:640] = lookup(kind, sigma_ref, SIGMA_SCALE, False)
     feat_ref[640:768] = jnp.where(present, lookup(kind, eps_ref, DEPTH_SCALE, True), 0.0)
-    feat_ref[768:896] = kind.astype(F32)
+    feat_ref[768:896] = jnp.zeros((128, 128), F32)
+    kick_ref[...] = lookup(kind, mass_ref, KICK_SCALE, False)
     low = jnp.logical_and(present, z < 0.5 * CELL_HEIGHT).astype(F32)
     high = jnp.logical_and(present, z >= 0.5 * CELL_HEIGHT).astype(F32)
     upto = (row <= lane).astype(F32).astype(BF16)
@@ -125,6 +150,9 @@
 
     lax.fori_loop(0, EXT, one, 0, unroll=4)
     clear(acc_ref, own_ref)
+    work = (fj_ref, (lead0_ref, lead1_ref), (sum0_ref, sum1_ref), acc_ref, own_ref)
+    if FIRST:
+        plane_patches(0, FIRST, *work)
     pl.semaphore_wait(barrier, 1)
     copy = pltpu.make_async_remote_copy(
         src_ref=fj_ref,
@@ -135,7 +163,7 @@
         device_id_type=MESH,
     )
     copy.start()
-    plane_patches(0, FIRST, fj_ref, (lead0_ref, lead1_ref), (sum0_ref, sum1_ref), acc_ref, own_ref)
+    plane_patches(FIRST, SECOND, *work)
     add_folded(acc_ref, own_ref)
     copy.wait()
 
@@ -148,24 +176,26 @@
         lead_ref[f] = jnp.broadcast_to(turned[128 - rows : 128, f : f + 1], (rows, 128))
 
 
-def pair_block(lead_ref, cols, same):
-    rows = lead_ref.shape[1]
-    delta = [lead_ref[d] - cols[d : d + 1] for d in range(3)]
+def pair_block(lead_ref, cols, keep=None, rows=slice(None)):
+    delta = [lead_ref[d, rows] - cols[d : d + 1] for d in range(3)]
     v = delta[0] * delta[0] + delta[1] * delta[1] + delta[2] * delta[2]
     w = lax.rsqrt(v)
     w2 = w * w
-    u = (lead_ref[4] + cols[4:5]) * w
+    u = (lead_ref[4, rows] + cols[4:5]) * w
     u = u * u
     u = u * u * u
     screened = (1.0 - lax.erf(v * w)) * w + GAUSS * jnp.exp2(v * (-LOG2E))
-    both = (lead_ref[5] * cols[5:6]) * (u * u - u) + (lead_ref[3] * cols[3:4]) * screened
-    keep = v < CUT
-    if same:
-        i = lax.broadcasted_iota(jnp.int32, (rows, 128), 0)
-        j = lax.broadcasted_iota(jnp.int32, (rows, 128), 1)
-        keep = jnp.logical_and(keep, i != j)
-    force = jnp.where(keep, both * w2, 0.0)
+    both = (lead_ref[5, rows] * cols[5:6]) * (u * u - u) + (lead_ref[3, rows] * cols[3:4]) * screened
+    near = v < CUT
+    if keep is not None:
+        near = jnp.logical_and(near, keep)
+    force = jnp.where(near, both * w2, 0.0)
     return [force * t for t in delta]
+
+
+def others_than(rows, start):
+    i = lax.broadcasted_iota(jnp.int32, (rows, 128), 0) + start
+    return i != lax.broadcasted_iota(jnp.int32, (rows, 128), 1)
 
 
 def fold8(value):
@@ -185,15 +215,19 @@
     x = k % PX
     left = ia - x + (x + PX - 1) % PX
     right = ia - x + (x + 1) % PX
-    kinds = ((0, 0, ia), (1, 0, right), (-1, 1, left + PX), (0, 1, ia + PX), (1, 1, right + PX))
-    for n, (sx, sy, b) in enumerate(kinds):
-        pull = pair_block(lead_ref, moved(fj_ref[b], STEP_W * sx, STEP_W * sy, 0.0), n == 0)
+    for n, (sx, sy, b) in enumerate(((1, 0, right), (-1, 1, left + PX), (0, 1, ia + PX), (1, 1, right + PX))):
+        pull = pair_block(lead_ref, moved(fj_ref[b], STEP_W * sx, STEP_W * sy, 0.0))
         for d in range(3):
             if n == 0:
                 sum_ref[d] = pull[d]
             else:
                 sum_ref[d] += pull[d]
-                acc_ref[b, 8 * d : 8 * d + 8, :] -= fold8(pull[d])
+            acc_ref[b, 8 * d : 8 * d + 8, :] -= fold8(pull[d])
+    half = lax.broadcasted_iota(jnp.int32, (8, 128), 1) < 64
+    pull = pair_block(lead_ref, fj_ref[ia], others_than(64, 0), slice(0, 64))
+    for d in range(3):
+        sum_ref[d, 0:64] += pull[d]
+        acc_ref[ia, 8 * d : 8 * d + 8, :] -= jnp.where(half, 0.0, fold8(pull[d]))
 
 
 def plane_patches(start, stop, fj_ref, leads, sums, acc_ref, own_ref):
@@ -276,8 +310,8 @@
                     r, rx, ry = near[n + 1]
                     cols = jnp.where(half, cols, moved(turn_ref[r], rx, ry, STEP_H))
                 else:
-                    cols = jnp.where(jnp.logical_or(half, row8 > 0), cols, -FAR)
-                pull = pair_block(lead_ref, cols, False)
+                    cols = jnp.where(half, cols, fj_ref[k + PX])
+                pull = pair_block(lead_ref, cols, others_than(64, 64) if n == 8 else None)
                 for d in range(3):
                     if n == 0:
                         sum_ref[d] = pull[d]
@@ -290,28 +324,35 @@
 
         def two(t, carry):
             k = 2 * t
-            for n in range(2):
-                patch(k + n, leads[n], sums[n])
-                spread(fj_ref[k + n + 2 + PX], leads[n], 64)
-                finish(k + n, sums[n], 64)
+            spread(fj_ref[k + 1 + PX], leads[1], 64)
+            finish((k + OWN - 1) % OWN, sums[1], 64)
+            patch(k, leads[0], sums[0])
+            spread(fj_ref[k + 2 + PX], leads[0], 64)
+            finish(k, sums[0], 64)
+            patch(k + 1, leads[1], sums[1])
             return carry
 
         spread(fj_ref[PX], leads[0], 64)
-        spread(fj_ref[PX + 1], leads[1], 64)
+        sum1_ref[...] = jnp.zeros(sum1_ref.shape, F32)
         lax.fori_loop(0, OWN // 2, two, 0)
+        finish(OWN - 1, sums[1], 64)
 
     @pl.when(spill)
     def _():
         def one(k, carry):
             spread(fj_ref[k + PX], full_ref, 128)
+            cols = jnp.where(jnp.logical_and(half, row8 == 0), -FAR, fj_ref[k + PX])
             for n, (p, px, py) in enumerate(others(k)):
-                pull = pair_block(full_ref, moved(fu_ref[p], px, py, STEP_H), False)
+                pull = pair_block(full_ref, moved(fu_ref[p], px, py, STEP_H))
                 for d in range(3):
                     if n == 0:
                         sumf_ref[d] = pull[d]
                     else:
                         sumf_ref[d] += pull[d]
                     acc_ref[p, 8 * d : 8 * d + 8, :] -= fold8(pull[d])
+            pull = pair_block(full_ref, cols, others_than(64, 64), slice(64, 128))
+            for d in range(3):
+                sumf_ref[d, 64:128] += pull[d]
             finish(k, sumf_ref, 128)
             return carry
 
@@ -321,8 +362,10 @@
     def _():
         def one(p, carry):
             for d in range(3):
-                total = fold(acc_ref, p, d) + pltpu.roll(fold(accr_ref, p, d), 64, 1)
-                up_ref[d, pl.ds(p, 1), :] = jnp.where(half[0:1], total, 0.0)
+                rows = slice(8 * d, 8 * d + 8)
+                total = acc_ref[p, rows, :] + pltpu.roll(accr_ref[p, rows, :], 64, 1)
+                total = jnp.sum(jnp.where(half, total, 0.0), axis=0, keepdims=True)
+                up_ref[d, pl.ds(p, 1), :] = total
             return carry
 
         lax.fori_loop(0, EXT, one, 0, unroll=4)
@@ -337,18 +380,13 @@
         lax.fori_loop(0, EXT, one, 0)
 
 
-def kick_kernel(
+def last_kernel(
     fj_ref,
     first_ref,
     rise_ref,
     up_ref,
     rank_ref,
-    type_ref,
-    mass_ref,
-    vel_ref,
-    pos_ref,
-    new_vel_ref,
-    new_pos_ref,
+    force_ref,
     own_ref,
     lead0_ref,
     lead1_ref,
@@ -374,7 +412,7 @@
         pl.semaphore_signal(barrier, inc=1, device_id={"sub": peer}, device_id_type=MESH)
     clear(acc_ref, own_ref)
     work = (fj_ref, (lead0_ref, lead1_ref), (sum0_ref, sum1_ref), acc_ref, own_ref)
-    plane_patches(FIRST, SECOND, *work)
+    plane_patches(SECOND, THIRD, *work)
     pl.semaphore_wait(barrier, SUBS)
     raised = pltpu.make_async_remote_copy(
         src_ref=up_ref,
@@ -385,7 +423,7 @@
         device_id_type=MESH,
     )
     raised.start()
-    plane_patches(SECOND, OWN, *work)
+    plane_patches(THIRD, OWN, *work)
     add_folded(acc_ref, own_ref)
     for d in range(3):
         own_ref[d] += first_ref[d]
@@ -404,20 +442,21 @@
             parts_ref[me, d, pl.ds(k, 1), :] = total[d : d + 1, :]
         return carry
 
-    lax.fori_loop(0, EXT, unsort, 0, unroll=4)
     copies = []
-    for step in range(1, SUBS):
-        copy = pltpu.make_async_remote_copy(
-            src_ref=parts_ref.at[me],
-            dst_ref=parts_ref.at[me],
-            send_sem=part_send.at[step - 1],
-            recv_sem=part_recv.at[step - 1],
-            device_id={"sub": lax.rem(me + step, SUBS)},
-            device_id_type=MESH,
-        )
-        copy.start()
-        copies.append(copy)
-    kick = lookup(type_ref[...], mass_ref, KICK_SCALE, False)
+    for piece in range(PIECES):
+        rows = pl.ds(piece * (EXT // PIECES), EXT // PIECES)
+        lax.fori_loop(piece * (EXT // PIECES), (piece + 1) * (EXT // PIECES), unsort, 0, unroll=4)
+        for step in range(1, SUBS):
+            copy = pltpu.make_async_remote_copy(
+                src_ref=parts_ref.at[me, :, rows],
+                dst_ref=parts_ref.at[me, :, rows],
+                send_sem=part_send.at[piece, step - 1],
+                recv_sem=part_recv.at[piece, step - 1],
+                device_id={"sub": lax.rem(me + step, SUBS)},
+                device_id_type=MESH,
+            )
+            copy.start()
+            copies.append(copy)
     for copy in copies:
         copy.wait()
     for s in range(SUBS):
@@ -426,10 +465,7 @@
             head = parts_ref[(s + SUBS - 1) % SUBS, d, PX + OWN : EXT, :]
             tail = parts_ref[(s + 1) % SUBS, d, 0:PX, :]
             force = jnp.concatenate([force[0:8] + head, force[8:24], force[24:32] + tail], axis=0)
-            rows = slice(s * OWN, (s + 1) * OWN)
-            velocity = vel_ref[d, rows, :] + kick[rows] * force
-            new_vel_ref[d, rows, :] = velocity
-            new_pos_ref[d, rows, :] = pos_ref[d, rows, :] + velocity
+            force_ref[d, s * OWN : (s + 1) * OWN, :] = force
 
 
 VM = pl.BlockSpec(memory_space=pltpu.VMEM)
@@ -445,19 +481,34 @@
     return [lead, lead, total, total, pltpu.VMEM((EXT, 24, 128), F32)]
 
 
-def first_call(positions, charges, atom_type, patch_fill, sigma_table, eps_table):
+def first_call(atoms, patch_fill, *tables):
     return pl.pallas_call(
         first_kernel,
-        out_shape=(shape(EXT, 8, 128), shape(EXT, 8, 128), shape(EXT, 128), shape(3, EXT, 128)),
-        in_specs=[VM] * 6,
-        out_specs=(VM, VM, VM, VM),
+        out_shape=(
+            shape(EXT, 8, 128),
+            shape(EXT, 8, 128),
+            shape(EXT, 128),
+            shape(3, EXT, 128),
+            shape(128, 128),
+        ),
+        in_specs=[pl.BlockSpec(memory_space=pltpu.HBM)] * 5,
+        out_specs=(VM,) * 5,
         scratch_shapes=[pltpu.VMEM((1024, 128), F32), pltpu.VMEM((128, 128), F32)]
         + work_shapes(128)
-        + [pltpu.SemaphoreType.DMA, pltpu.SemaphoreType.DMA],
+        + [
+            pltpu.VMEM((5, 128, 128), F32),
+            pltpu.VMEM((1, 128), jnp.int32),
+            pltpu.VMEM((1, 8), F32),
+            pltpu.VMEM((1, 8), F32),
+            pltpu.VMEM((1, 8), F32),
+            pltpu.SemaphoreType.DMA((5,)),
+            pltpu.SemaphoreType.DMA,
+            pltpu.SemaphoreType.DMA,
+        ],
         compiler_params=pltpu.CompilerParams(
             vmem_limit_bytes=VMEM_BYTES, collective_id=0, has_side_effects=True
         ),
-    )(positions, charges, atom_type, patch_fill[None], sigma_table[None], eps_table[None])
+    )(atoms, patch_fill[None], *(table[None] for table in tables))
 
 
 def up_call(features, above):
@@ -473,12 +524,12 @@
     )(features, above)
 
 
-def kick_call(features, first, rise, up, rank, atom_type, inv_mass_table, velocities, positions):
+def last_call(features, first, rise, up, rank):
     return pl.pallas_call(
-        kick_kernel,
-        out_shape=(shape(3, 128, 128), shape(3, 128, 128)),
-        in_specs=[VM] * 9,
-        out_specs=(VM, VM),
+        last_kernel,
+        out_shape=shape(3, 128, 128),
+        in_specs=[VM] * 5,
+        out_specs=VM,
         scratch_shapes=[pltpu.VMEM((3, EXT, 128), F32)]
         + work_shapes(128)
         + [
@@ -486,13 +537,13 @@
             pltpu.VMEM((SUBS, 3, EXT, 128), F32),
             pltpu.SemaphoreType.DMA,
             pltpu.SemaphoreType.DMA,
-            pltpu.SemaphoreType.DMA((SUBS - 1,)),
-            pltpu.SemaphoreType.DMA((SUBS - 1,)),
+            pltpu.SemaphoreType.DMA((PIECES, SUBS - 1)),
+            pltpu.SemaphoreType.DMA((PIECES, SUBS - 1)),
         ],
         compiler_params=pltpu.CompilerParams(
             vmem_limit_bytes=VMEM_BYTES, collective_id=1, has_side_effects=True
         ),
-    )(features, first, rise, up, rank, atom_type, inv_mass_table[None], velocities, positions)
+    )(features, first, rise, up, rank)
 
 
 def local(
@@ -507,11 +558,15 @@
     pair_first,
     pair_second,
 ):
-    features, above, rank, first = first_call(
-        positions, charges, atom_type, patch_fill, sigma_table, eps_table
+    atoms = jnp.concatenate([positions, charges[None], atom_type.astype(F32)[None]])
+    features, above, rank, first, kick = first_call(
+        atoms, patch_fill, sigma_table, eps_table, inv_mass_table
     )
     up, rise = up_call(features, above)
-    return kick_call(features, first, rise, up, rank, atom_type, inv_mass_table, velocities, positions)
+    forces = last_call(features, first, rise, up, rank)
+    new_velocities = velocities + kick[None] * forces
+    new_positions = positions + new_velocities
+    return (new_velocities, new_positions)
 
 
 def solution(mesh):

time: 54.3 us -> 47.1 us (0.87)
  local copies, waits for them, and re-layouts: 5.26 us -> 0.04 us
  Pallas kernels: 48.1 us -> 43.6 us
  other arithmetic: 0 us -> 2.64 us
    unnamed x22 -> x14, local copies, waits for them, and re-layouts: 5.26 us -> 0.04 us
    pallas_call x1, Pallas kernels: 17.3 us -> 12.8 us  [first_call(): pl.pallas_call(first_kernel, out_shape=(shape(EXT, 8, 128), shape(EXT, 8,...]
    pallas_call x1, Pallas kernels: 14.7 us -> 12.8 us  [up_call(): pl.pallas_call(up_kernel, out_shape=(shape(3, EXT, 128), shape(3, OWN, 12...]
    pallas_call x1, Pallas kernels: 16.1 us -> 18 us  [last_call(): pl.pallas_call(last_kernel, out_shape=shape(3, 128, 128), in_specs=[VM] *...]
    concatenate x0 -> x1, other arithmetic: none -> 0.97 us  [local(): jnp.concatenate([positions, charges[None], atom_type.astype(F32)[None]])]
    broadcast_in_dim x0 -> x1, other arithmetic: none -> 0.88 us  [local(): atom_type.astype(F32)[None]]
    add x0 -> x1, other arithmetic: none -> 0.79 us  [local(): new_positions = positions + new_velocities]
where the time goes in v3:
time: 47.1 us; the launch traced here: 47 us
  Pallas kernels  43.6 us (93%)
  other arithmetic  2.64 us (6%)
  between operations  0.76 us (2%)
    pallas_call x1, Pallas kernels, last_call(): pl.pallas_call(last_kernel, out_shape=shape(3, 128, 128), in_specs=[VM] *...  18 us
    pallas_call x1, Pallas kernels, first_call(): pl.pallas_call(first_kernel, out_shape=(shape(EXT, 8, 128), shape(EXT, 8,...  12.8 us
    pallas_call x1, Pallas kernels, up_call(): pl.pallas_call(up_kernel, out_shape=(shape(3, EXT, 128), shape(3, OWN, 12...  12.8 us
    concatenate x1, other arithmetic, local(): jnp.concatenate([positions, charges[None], atom_type.astype(F32)[None]])  0.97 us

profile of v3, /device:TPU:2, one launch (start us, length us, event | category | flops | bytes accessed | tf_op | source)
XLA Modules:
  0.0 47.0 jit_solution(3856825929746324813)
XLA Ops:
  0.6 0.0 copy-start.6
  0.6 0.9 %convert_bitcast_fusion = f32[1,128,128]{2,1,0:T(8,128)S(1)} fusion(s32[128,128]{1,0:T(8,128)} %param.13), kind=kLoop, calls=%fused_computation.2 | loop fusion | flops 16384 | bytes 131072 | tf_op jit(solution)/shard_map/broadcast_in_dim | solution.py:561
  1.5 0.0 copy-done.6
  1.5 0.0 copy-start
  1.5 0.0 copy-start.1
  1.5 0.0 copy-start.2
  1.6 0.0 copy-start.3
  1.6 1.0 %pad_maximum_fusion.atom_hbm = f32[5,128,128]{2,1,0:T(8,128)S(1)} fusion(f32[1,128,128]{2,1,0:T(8,128)S(1)} %convert_bitcast_fusion, f32[1,128,128]{2,1,0:T(8,128)S(1)} %bitcast.11, f32[3,128,128]{2,1,0:T(8,128)} %param.10), kind=kLoop, calls=%fused_computation | loop fusion | flops 163840 | bytes 655360 | tf_op jit(solution)/shard_map/concatenate | solution.py:561
  2.5 0.0 copy-done
  2.5 0.0 copy-done.1
  2.6 0.0 copy-done.2
  2.6 0.0 copy-done.3
  2.6 12.8 %shard_map.95 = (f32[48,8,128]{2,1,0:T(8,128)S(1)}, f32[48,8,128]{2,1,0:T(8,128)S(1)}, f32[48,128]{1,0:T(8,128)S(1)}, f32[3,48,128]{2,1,0:T(8,128)S(1)}, f32[128,128]{1,0:T(8,128)S(1)}) custom-call(f32[5,128,128]{2,1,0:T(8,128)S(1)} %pad_maximum_fusion.atom_hbm, s32[1,128]{1,0:T(1,128)S(1)} %bitcast.7, f32[1,8]{1,0:T(1,128)S(1)} %bitcast.8, ...), custom_call_target="tpu_custom_call" | custom-call | tf_op jit(solution)/shard_map/pallas_call | solution.py:485
  15.4 12.8 %shard_map.96 = (f32[3,48,128]{2,1,0:T(8,128)S(1)}, f32[3,32,128]{2,1,0:T(8,128)S(1)}) custom-call(f32[48,8,128]{2,1,0:T(8,128)S(1)} %get-tuple-element.10.fj_ref, f32[48,8,128]{2,1,0:T(8,128)S(1)} %get-tuple-element.12.fu_ref), custom_call_target="tpu_custom_call" | custom-call | tf_op jit(solution)/shard_map/pallas_call | solution.py:515
  28.2 0.0 copy-start.4
  28.2 0.0 copy-start.5
  28.2 18.0 %shard_map.97 = f32[3,128,128]{2,1,0:T(8,128)S(1)} custom-call(f32[48,8,128]{2,1,0:T(8,128)S(1)} %get-tuple-element.10.fj_ref, f32[3,48,128]{2,1,0:T(8,128)S(1)} %get-tuple-element.11.first_ref, f32[3,32,128]{2,1,0:T(8,128)S(1)} %get-tuple-element.13.rise_ref, f32[3,48,128]{2,1,0:T(8,128)S(1)} %get-tuple-element.14.up_ref, ...), custom_call_target="tpu_custom_call" | custom-call | tf_op jit(solution)/shard_map/pallas_call | solution.py:528
  46.2 0.0 copy-done.4
  46.2 0.0 copy-done.5
  46.2 0.8 %fusion = (f32[3,128,128]{2,1,0:T(8,128)}, f32[3,128,128]{2,1,0:T(8,128)}) fusion(f32[3,128,128]{2,1,0:T(8,128)S(1)} %copy-done.4, f32[3,128,128]{2,1,0:T(8,128)S(1)} %copy-done.5, f32[3,128,128]{2,1,0:T(8,128)S(1)} %shard_map.97, f32[128,128]{1,0:T(8,128)S(1)} %get-tuple-element.9), kind=kLoop, calls=%fused_computation.3 | loop fusion | flops 147456 | bytes 1048576 | tf_op jit(solution)/shard_map/add | solution.py:568
Async XLA Ops:
  0.6 0.9 %copy-start.6 = (f32[128,128]{1,0:T(8,128)S(1)}, f32[128,128]{1,0:T(8,128)}, u32[]{:S(2)}) copy-start(f32[128,128]{1,0:T(8,128)} %param.12) | copy-start | bytes 196612
  1.5 1.0 %copy-start = (s32[128]{0:T(128)S(1)}, s32[128]{0:T(128)}, u32[]{:S(2)}) copy-start(s32[128]{0:T(128)} %param.14) | copy-start | bytes 1540
  1.5 1.0 %copy-start.1 = (f32[8]{0:T(128)S(1)}, f32[8]{0:T(128)}, u32[]{:S(2)}) copy-start(f32[8]{0:T(128)} %param.15) | copy-start | bytes 100
  1.5 1.0 %copy-start.2 = (f32[8]{0:T(128)S(1)}, f32[8]{0:T(128)}, u32[]{:S(2)}) copy-start(f32[8]{0:T(128)} %param.16) | copy-start | bytes 100
  1.6 1.0 %copy-start.3 = (f32[8]{0:T(128)S(1)}, f32[8]{0:T(128)}, u32[]{:S(2)}) copy-start(f32[8]{0:T(128)} %param.17) | copy-start | bytes 100
  28.2 18.0 %copy-start.4 = (f32[3,128,128]{2,1,0:T(8,128)S(1)}, f32[3,128,128]{2,1,0:T(8,128)}, u32[]{:S(2)}) copy-start(f32[3,128,128]{2,1,0:T(8,128)} %param.10) | copy-start | bytes 589828
  28.2 18.0 %copy-start.5 = (f32[3,128,128]{2,1,0:T(8,128)S(1)}, f32[3,128,128]{2,1,0:T(8,128)}, u32[]{:S(2)}) copy-start(f32[3,128,128]{2,1,0:T(8,128)} %param.11) | copy-start | bytes 589828

commit v4 on v3

--- a/solution.py
+++ b/solution.py
@@ -27,10 +27,10 @@
 DEPTH_SCALE = math.sqrt(12.0 * SPLIT_BETA)
 CHARGE_SCALE = math.sqrt(COULOMB * SPLIT_BETA * SPLIT_BETA)
 FAR = 1.0e4
-FIRST = 4
+FIRST = 6
 SECOND = 12
 THIRD = 20
-PIECES = 2
+PIECES = 3
 MESH = pl.DeviceIdType.MESH
 F32 = jnp.float32
 BF16 = jnp.bfloat16
@@ -148,7 +148,7 @@
         fj_ref[k] = total[0:8] + total[8:16] + total[16:24]
         return carry
 
-    lax.fori_loop(0, EXT, one, 0, unroll=4)
+    lax.fori_loop(0, EXT, one, 0, unroll=16)
     clear(acc_ref, own_ref)
     work = (fj_ref, (lead0_ref, lead1_ref), (sum0_ref, sum1_ref), acc_ref, own_ref)
     if FIRST:
@@ -233,11 +233,14 @@
 def plane_patches(start, stop, fj_ref, leads, sums, acc_ref, own_ref):
     def two(t, carry):
         k = start + 2 * t
-        for n in range(2):
-            plane_patch(k + n, fj_ref, leads[n], sums[n], acc_ref)
-            spread(fj_ref[k + n + 2 + PX], leads[n], 128)
-            for d in range(3):
-                own_ref[d, pl.ds(k + n + PX, 1), :] = jnp.sum(sums[n][d].T, axis=0, keepdims=True)
+        plane_patch(k, fj_ref, leads[0], sums[0], acc_ref)
+        spread(fj_ref[k + 2 + PX], leads[0], 128)
+        plane_patch(k + 1, fj_ref, leads[1], sums[1], acc_ref)
+        for d in range(3):
+            own_ref[d, pl.ds(k + PX, 1), :] = jnp.sum(sums[0][d].T, axis=0, keepdims=True)
+        spread(fj_ref[k + 3 + PX], leads[1], 128)
+        for d in range(3):
+            own_ref[d, pl.ds(k + 1 + PX, 1), :] = jnp.sum(sums[1][d].T, axis=0, keepdims=True)
         return carry
 
     spread(fj_ref[start + PX], leads[0], 128)
@@ -250,7 +253,7 @@
         acc_ref[k] = jnp.zeros((24, 128), F32)
         return carry
 
-    lax.fori_loop(0, EXT, one, 0, unroll=4)
+    lax.fori_loop(0, EXT, one, 0, unroll=16)
     own_ref[...] = jnp.zeros(own_ref.shape, F32)
 
 
@@ -264,7 +267,7 @@
             own_ref[d, pl.ds(k, 1), :] += fold(acc_ref, k, d)
         return carry
 
-    lax.fori_loop(PX, EXT, one, 0, unroll=4)
+    lax.fori_loop(PX, EXT, one, 0, unroll=8)
 
 
 def up_kernel(
@@ -274,7 +277,6 @@
     row8 = lax.broadcasted_iota(jnp.int32, (8, 128), 0)
     half = lane8 < 64
     leads = (lead0_ref, lead1_ref)
-    sums = (sum0_ref, sum1_ref)
     sides = [(dr, dx) for dr in (-1, 0, 1) for dx in (-1, 0, 1)]
 
     def start(p, worst):
@@ -284,7 +286,7 @@
         accr_ref[p] = jnp.zeros((24, 128), F32)
         return jnp.maximum(worst, jnp.maximum(tile[7:8], fj_ref[p, 7:8, :]))
 
-    worst = lax.fori_loop(0, EXT, start, jnp.zeros((1, 128), F32), unroll=4)
+    worst = lax.fori_loop(0, EXT, start, jnp.zeros((1, 128), F32), unroll=8)
     spill = jnp.max(worst) > 0.0
 
     def others(k):
@@ -301,7 +303,7 @@
 
     @pl.when(jnp.logical_not(spill))
     def _():
-        def patch(k, lead_ref, sum_ref):
+        def patch(k, lead_ref, rows):
             near = others(k)
             for n in range(0, 9, 2):
                 p, px, py = near[n]
@@ -314,28 +316,33 @@
                 pull = pair_block(lead_ref, cols, others_than(64, 64) if n == 8 else None)
                 for d in range(3):
                     if n == 0:
-                        sum_ref[d] = pull[d]
+                        sumf_ref[d, rows] = pull[d]
                     else:
-                        sum_ref[d] += pull[d]
+                        sumf_ref[d, rows] += pull[d]
                     back = fold8(pull[d])
                     acc_ref[p, 8 * d : 8 * d + 8, :] -= back
                     if n < 8:
                         accr_ref[r, 8 * d : 8 * d + 8, :] -= back
 
+        def finish_two(k):
+            for d in range(3):
+                total = jnp.sum(sumf_ref[d].T, axis=0, keepdims=True)
+                own_ref[d, pl.ds(k, 1), :] = jnp.where(half[0:1], 0.0, pltpu.roll(total, 64, 1))
+                own_ref[d, pl.ds(k + 1, 1), :] = jnp.where(half[0:1], 0.0, total)
+
         def two(t, carry):
             k = 2 * t
             spread(fj_ref[k + 1 + PX], leads[1], 64)
-            finish((k + OWN - 1) % OWN, sums[1], 64)
-            patch(k, leads[0], sums[0])
+            finish_two((k + OWN - 2) % OWN)
+            patch(k, leads[0], slice(0, 64))
             spread(fj_ref[k + 2 + PX], leads[0], 64)
-            finish(k, sums[0], 64)
-            patch(k + 1, leads[1], sums[1])
+            patch(k + 1, leads[1], slice(64, 128))
             return carry
 
         spread(fj_ref[PX], leads[0], 64)
-        sum1_ref[...] = jnp.zeros(sum1_ref.shape, F32)
+        sumf_ref[...] = jnp.zeros(sumf_ref.shape, F32)
         lax.fori_loop(0, OWN // 2, two, 0)
-        finish(OWN - 1, sums[1], 64)
+        finish_two(OWN - 2)
 
     @pl.when(spill)
     def _():
@@ -368,7 +375,7 @@
                 up_ref[d, pl.ds(p, 1), :] = total
             return carry
 
-        lax.fori_loop(0, EXT, one, 0, unroll=4)
+        lax.fori_loop(0, EXT, one, 0, unroll=16)
 
     @pl.when(spill)
     def _():
@@ -445,7 +452,7 @@
     copies = []
     for piece in range(PIECES):
         rows = pl.ds(piece * (EXT // PIECES), EXT // PIECES)
-        lax.fori_loop(piece * (EXT // PIECES), (piece + 1) * (EXT // PIECES), unsort, 0, unroll=4)
+        lax.fori_loop(piece * (EXT // PIECES), (piece + 1) * (EXT // PIECES), unsort, 0, unroll=16)
         for step in range(1, SUBS):
             copy = pltpu.make_async_remote_copy(
                 src_ref=parts_ref.at[me, :, rows],
@@ -558,7 +565,9 @@
     pair_first,
     pair_second,
 ):
-    atoms = jnp.concatenate([positions, charges[None], atom_type.astype(F32)[None]])
+    plane = lax.broadcasted_iota(jnp.int32, (5, 128, 128), 0)
+    atoms = jnp.where(plane == 3, charges[None], atom_type.astype(F32)[None])
+    atoms = jnp.where(plane < 3, jnp.pad(positions, ((0, 2), (0, 0), (0, 0))), atoms)
     features, above, rank, first, kick = first_call(
         atoms, patch_fill, sigma_table, eps_table, inv_mass_table
     )

time: 47.1 us -> 44.2 us (0.938); the launches traced: 47 us -> 43.6 us
  Pallas kernels: 43.6 us -> 40 us
    pallas_call x1, Pallas kernels: 12.8 us -> 11.1 us  [up_call(): pl.pallas_call(up_kernel, out_shape=(shape(3, EXT, 128), shape(3, OWN, 12...]
    pallas_call x1, Pallas kernels: 12.8 us -> 11.7 us  [first_call(): pl.pallas_call(first_kernel, out_shape=(shape(EXT, 8, 128), shape(EXT, 8,...]
    select_n x0 -> x1, other arithmetic: none -> 1.05 us  [local(): jnp.where(plane < 3, jnp.pad(positions, ((0, 2), (0, 0), (0, 0))), atoms)]
    concatenate x1 -> x0, other arithmetic: 0.97 us -> none  [local(): jnp.concatenate([positions, charges[None], atom_type.astype(F32)[None]])]
    convert_element_type x0 -> x1, other arithmetic: none -> 0.88 us  [local(): atoms = jnp.where(plane == 3, charges[None], atom_type.astype(F32)[None])]
    broadcast_in_dim x1 -> x0, other arithmetic: 0.88 us -> none  [local(): atom_type.astype(F32)[None]]
    pallas_call x1, Pallas kernels: 18 us -> 17.2 us  [last_call(): pl.pallas_call(last_kernel, out_shape=shape(3, 128, 128), in_specs=[VM] *...]
where the time goes in v4:
time: 44.2 us; the launch traced here: 43.6 us
  Pallas kernels  40 us (90%)
  other arithmetic  2.72 us (6%)
  between operations  0.77 us (2%)
    pallas_call x1, Pallas kernels, last_call(): pl.pallas_call(last_kernel, out_shape=shape(3, 128, 128), in_specs=[VM] *...  17.2 us
    pallas_call x1, Pallas kernels, first_call(): pl.pallas_call(first_kernel, out_shape=(shape(EXT, 8, 128), shape(EXT, 8,...  11.7 us
    pallas_call x1, Pallas kernels, up_call(): pl.pallas_call(up_kernel, out_shape=(shape(3, EXT, 128), shape(3, OWN, 12...  11.1 us
    select_n x1, other arithmetic, local(): jnp.where(plane < 3, jnp.pad(positions, ((0, 2), (0, 0), (0, 0))), atoms)  1.05 us

profile of v4, /device:TPU:2, one launch (start us, length us, event | category | flops | bytes accessed | tf_op | source)
XLA Modules:
  0.0 43.6 jit_solution(6348981768108557083)
XLA Ops:
  0.6 0.0 copy-start.6
  0.7 0.9 %convert_element_type.5 = f32[128,128]{1,0:T(8,128)S(1)} convert(s32[128,128]{1,0:T(8,128)} %param.13) | non-fusion elementwise | flops 16384 | bytes 131072 | tf_op jit(solution)/shard_map/convert_element_type | solution.py:569
  1.5 0.0 copy-done.6
  1.5 0.0 copy-start
  1.5 0.0 copy-start.1
  1.6 0.0 copy-start.2
  1.6 0.0 copy-start.3
  1.6 1.0 %select_select_fusion.atom_hbm = f32[5,128,128]{2,1,0:T(8,128)S(1)} fusion(f32[3,128,128]{2,1,0:T(8,128)} %param.10, f32[128,128]{1,0:T(8,128)S(1)} %convert_element_type.5, f32[128,128]{1,0:T(8,128)S(1)} %copy-done.6, pred[5]{0:T(512)(128)(4,1)S(1)} %get-tuple-element.18, pred[5]{0:T(512)(128)(4,1)S(1)} %get-tuple-element.19), kind=kLoop, calls=%fused_computation | loop fusion | flops 163840 | bytes 655370 | tf_op jit(solution)/shard_map/jit(_where)/select_n | solution.py:570
  2.6 0.0 copy-done
  2.6 0.0 copy-done.1
  2.7 0.0 copy-done.2
  2.7 0.0 copy-done.3
  2.7 11.7 %shard_map.95 = (f32[48,8,128]{2,1,0:T(8,128)S(1)}, f32[48,8,128]{2,1,0:T(8,128)S(1)}, f32[48,128]{1,0:T(8,128)S(1)}, f32[3,48,128]{2,1,0:T(8,128)S(1)}, f32[128,128]{1,0:T(8,128)S(1)}) custom-call(f32[5,128,128]{2,1,0:T(8,128)S(1)} %select_select_fusion.atom_hbm, s32[1,128]{1,0:T(1,128)S(1)} %bitcast.4, f32[1,8]{1,0:T(1,128)S(1)} %bitcast.5, ...), custom_call_target="tpu_custom_call" | custom-call | tf_op jit(solution)/shard_map/pallas_call | solution.py:492
  14.4 11.1 %shard_map.96 = (f32[3,48,128]{2,1,0:T(8,128)S(1)}, f32[3,32,128]{2,1,0:T(8,128)S(1)}) custom-call(f32[48,8,128]{2,1,0:T(8,128)S(1)} %get-tuple-element.10.fj_ref, f32[48,8,128]{2,1,0:T(8,128)S(1)} %get-tuple-element.12.fu_ref), custom_call_target="tpu_custom_call" | custom-call | tf_op jit(solution)/shard_map/pallas_call | solution.py:522
  25.5 0.0 copy-start.4
  25.5 0.0 copy-start.5
  25.6 17.2 %shard_map.97 = f32[3,128,128]{2,1,0:T(8,128)S(1)} custom-call(f32[48,8,128]{2,1,0:T(8,128)S(1)} %get-tuple-element.10.fj_ref, f32[3,48,128]{2,1,0:T(8,128)S(1)} %get-tuple-element.11.first_ref, f32[3,32,128]{2,1,0:T(8,128)S(1)} %get-tuple-element.13.rise_ref, f32[3,48,128]{2,1,0:T(8,128)S(1)} %get-tuple-element.14.up_ref, ...), custom_call_target="tpu_custom_call" | custom-call | tf_op jit(solution)/shard_map/pallas_call | solution.py:535
  42.8 0.0 copy-done.4
  42.8 0.0 copy-done.5
  42.8 0.8 %fusion = (f32[3,128,128]{2,1,0:T(8,128)}, f32[3,128,128]{2,1,0:T(8,128)}) fusion(f32[3,128,128]{2,1,0:T(8,128)S(1)} %copy-done.4, f32[3,128,128]{2,1,0:T(8,128)S(1)} %copy-done.5, f32[3,128,128]{2,1,0:T(8,128)S(1)} %shard_map.97, f32[128,128]{1,0:T(8,128)S(1)} %get-tuple-element.9), kind=kLoop, calls=%fused_computation.4 | loop fusion | flops 147456 | bytes 1048576 | tf_op jit(solution)/shard_map/add | solution.py:577
  (1 shorter events, 0.0 us)
Async XLA Ops:
  0.6 0.9 %copy-start.6 = (f32[128,128]{1,0:T(8,128)S(1)}, f32[128,128]{1,0:T(8,128)}, u32[]{:S(2)}) copy-start(f32[128,128]{1,0:T(8,128)} %param.12) | copy-start | bytes 196612
  1.5 1.1 %copy-start = (s32[128]{0:T(128)S(1)}, s32[128]{0:T(128)}, u32[]{:S(2)}) copy-start(s32[128]{0:T(128)} %param.14) | copy-start | bytes 1540
  1.5 1.1 %copy-start.1 = (f32[8]{0:T(128)S(1)}, f32[8]{0:T(128)}, u32[]{:S(2)}) copy-start(f32[8]{0:T(128)} %param.15) | copy-start | bytes 100
  1.6 1.1 %copy-start.2 = (f32[8]{0:T(128)S(1)}, f32[8]{0:T(128)}, u32[]{:S(2)}) copy-start(f32[8]{0:T(128)} %param.16) | copy-start | bytes 100
  1.6 1.1 %copy-start.3 = (f32[8]{0:T(128)S(1)}, f32[8]{0:T(128)}, u32[]{:S(2)}) copy-start(f32[8]{0:T(128)} %param.17) | copy-start | bytes 100
  25.5 17.2 %copy-start.4 = (f32[3,128,128]{2,1,0:T(8,128)S(1)}, f32[3,128,128]{2,1,0:T(8,128)}, u32[]{:S(2)}) copy-start(f32[3,128,128]{2,1,0:T(8,128)} %param.10) | copy-start | bytes 589828
  25.5 17.2 %copy-start.5 = (f32[3,128,128]{2,1,0:T(8,128)S(1)}, f32[3,128,128]{2,1,0:T(8,128)}, u32[]{:S(2)}) copy-start(f32[3,128,128]{2,1,0:T(8,128)} %param.11) | copy-start | bytes 589828

commit v5 on v4

--- a/solution.py
+++ b/solution.py
@@ -267,7 +267,7 @@
             own_ref[d, pl.ds(k, 1), :] += fold(acc_ref, k, d)
         return carry
 
-    lax.fori_loop(PX, EXT, one, 0, unroll=8)
+    lax.fori_loop(PX, EXT, one, 0, unroll=20)
 
 
 def up_kernel(
@@ -286,7 +286,7 @@
         accr_ref[p] = jnp.zeros((24, 128), F32)
         return jnp.maximum(worst, jnp.maximum(tile[7:8], fj_ref[p, 7:8, :]))
 
-    worst = lax.fori_loop(0, EXT, start, jnp.zeros((1, 128), F32), unroll=8)
+    worst = lax.fori_loop(0, EXT, start, jnp.zeros((1, 128), F32), unroll=16)
     spill = jnp.max(worst) > 0.0
 
     def others(k):

time: 44.2 us -> 44 us (level)
  no operation moved by 1% of the time
where the time goes in v5:
time: 44 us; the launch traced here: 43.4 us
  Pallas kernels  39.8 us (90%)
  other arithmetic  2.72 us (6%)
  between operations  0.77 us (2%)
    pallas_call x1, Pallas kernels, last_call(): pl.pallas_call(last_kernel, out_shape=shape(3, 128, 128), in_specs=[VM] *...  17.2 us
    pallas_call x1, Pallas kernels, first_call(): pl.pallas_call(first_kernel, out_shape=(shape(EXT, 8, 128), shape(EXT, 8,...  11.7 us
    pallas_call x1, Pallas kernels, up_call(): pl.pallas_call(up_kernel, out_shape=(shape(3, EXT, 128), shape(3, OWN, 12...  10.9 us
    select_n x1, other arithmetic, local(): jnp.where(plane < 3, jnp.pad(positions, ((0, 2), (0, 0), (0, 0))), atoms)  1.05 us

profile of v5, /device:TPU:2, one launch (start us, length us, event | category | flops | bytes accessed | tf_op | source)
XLA Modules:
  0.0 43.4 jit_solution(5937084376853387607)
XLA Ops:
  0.6 0.0 copy-start.6
  0.7 0.9 %convert_element_type.5 = f32[128,128]{1,0:T(8,128)S(1)} convert(s32[128,128]{1,0:T(8,128)} %param.13) | non-fusion elementwise | flops 16384 | bytes 131072 | tf_op jit(solution)/shard_map/convert_element_type | solution.py:569
  1.5 0.0 copy-done.6
  1.5 0.0 copy-start
  1.5 0.0 copy-start.1
  1.6 0.0 copy-start.2
  1.6 0.0 copy-start.3
  1.6 1.0 %select_select_fusion.atom_hbm = f32[5,128,128]{2,1,0:T(8,128)S(1)} fusion(f32[3,128,128]{2,1,0:T(8,128)} %param.10, f32[128,128]{1,0:T(8,128)S(1)} %convert_element_type.5, f32[128,128]{1,0:T(8,128)S(1)} %copy-done.6, pred[5]{0:T(512)(128)(4,1)S(1)} %get-tuple-element.18, pred[5]{0:T(512)(128)(4,1)S(1)} %get-tuple-element.19), kind=kLoop, calls=%fused_computation | loop fusion | flops 163840 | bytes 655370 | tf_op jit(solution)/shard_map/jit(_where)/select_n | solution.py:570
  2.6 0.0 copy-done
  2.6 0.0 copy-done.1
  2.7 0.0 copy-done.2
  2.7 0.0 copy-done.3
  2.7 11.7 %shard_map.95 = (f32[48,8,128]{2,1,0:T(8,128)S(1)}, f32[48,8,128]{2,1,0:T(8,128)S(1)}, f32[48,128]{1,0:T(8,128)S(1)}, f32[3,48,128]{2,1,0:T(8,128)S(1)}, f32[128,128]{1,0:T(8,128)S(1)}) custom-call(f32[5,128,128]{2,1,0:T(8,128)S(1)} %select_select_fusion.atom_hbm, s32[1,128]{1,0:T(1,128)S(1)} %bitcast.4, f32[1,8]{1,0:T(1,128)S(1)} %bitcast.5, ...), custom_call_target="tpu_custom_call" | custom-call | tf_op jit(solution)/shard_map/pallas_call | solution.py:492
  14.4 10.9 %shard_map.96 = (f32[3,48,128]{2,1,0:T(8,128)S(1)}, f32[3,32,128]{2,1,0:T(8,128)S(1)}) custom-call(f32[48,8,128]{2,1,0:T(8,128)S(1)} %get-tuple-element.10.fj_ref, f32[48,8,128]{2,1,0:T(8,128)S(1)} %get-tuple-element.12.fu_ref), custom_call_target="tpu_custom_call" | custom-call | tf_op jit(solution)/shard_map/pallas_call | solution.py:522
  25.3 0.0 copy-start.4
  25.3 0.0 copy-start.5
  25.4 17.2 %shard_map.97 = f32[3,128,128]{2,1,0:T(8,128)S(1)} custom-call(f32[48,8,128]{2,1,0:T(8,128)S(1)} %get-tuple-element.10.fj_ref, f32[3,48,128]{2,1,0:T(8,128)S(1)} %get-tuple-element.11.first_ref, f32[3,32,128]{2,1,0:T(8,128)S(1)} %get-tuple-element.13.rise_ref, f32[3,48,128]{2,1,0:T(8,128)S(1)} %get-tuple-element.14.up_ref, ...), custom_call_target="tpu_custom_call" | custom-call | tf_op jit(solution)/shard_map/pallas_call | solution.py:535
  42.6 0.0 copy-done.4
  42.6 0.0 copy-done.5
  42.6 0.8 %fusion = (f32[3,128,128]{2,1,0:T(8,128)}, f32[3,128,128]{2,1,0:T(8,128)}) fusion(f32[3,128,128]{2,1,0:T(8,128)S(1)} %copy-done.4, f32[3,128,128]{2,1,0:T(8,128)S(1)} %copy-done.5, f32[3,128,128]{2,1,0:T(8,128)S(1)} %shard_map.97, f32[128,128]{1,0:T(8,128)S(1)} %get-tuple-element.9), kind=kLoop, calls=%fused_computation.4 | loop fusion | flops 147456 | bytes 1048576 | tf_op jit(solution)/shard_map/add | solution.py:577
  (1 shorter events, 0.0 us)
Async XLA Ops:
  0.6 0.9 %copy-start.6 = (f32[128,128]{1,0:T(8,128)S(1)}, f32[128,128]{1,0:T(8,128)}, u32[]{:S(2)}) copy-start(f32[128,128]{1,0:T(8,128)} %param.12) | copy-start | bytes 196612
  1.5 1.1 %copy-start = (s32[128]{0:T(128)S(1)}, s32[128]{0:T(128)}, u32[]{:S(2)}) copy-start(s32[128]{0:T(128)} %param.14) | copy-start | bytes 1540
  1.5 1.1 %copy-start.1 = (f32[8]{0:T(128)S(1)}, f32[8]{0:T(128)}, u32[]{:S(2)}) copy-start(f32[8]{0:T(128)} %param.15) | copy-start | bytes 100
  1.6 1.1 %copy-start.2 = (f32[8]{0:T(128)S(1)}, f32[8]{0:T(128)}, u32[]{:S(2)}) copy-start(f32[8]{0:T(128)} %param.16) | copy-start | bytes 100
  1.6 1.1 %copy-start.3 = (f32[8]{0:T(128)S(1)}, f32[8]{0:T(128)}, u32[]{:S(2)}) copy-start(f32[8]{0:T(128)} %param.17) | copy-start | bytes 100
  25.3 17.2 %copy-start.4 = (f32[3,128,128]{2,1,0:T(8,128)S(1)}, f32[3,128,128]{2,1,0:T(8,128)}, u32[]{:S(2)}) copy-start(f32[3,128,128]{2,1,0:T(8,128)} %param.10) | copy-start | bytes 589828
  25.3 17.2 %copy-start.5 = (f32[3,128,128]{2,1,0:T(8,128)S(1)}, f32[3,128,128]{2,1,0:T(8,128)}, u32[]{:S(2)}) copy-start(f32[3,128,128]{2,1,0:T(8,128)} %param.11) | copy-start | bytes 589828
